TPU v7x, 32 devices: a whole 2x2x4 slice. The times are simulated.
32 devices in a mesh: half: 2 (over y), dp: 8 (over z, x), mp: 2 (over core).
Axes of the slice: x: 2, y: 2, z: 4, core: 2. Of those that a mesh axis runs over, the one named last changes fastest.
Arguments:
- tokens: bfloat16 [2, 9216, 768], P('half', 'dp'), may hold values from -6 to 6
- qkv_weight: bfloat16 [2, 768, 3, 768], P('half', None, None, 'mp'), may hold values from -0.21875 to 0.21875
- out_weight: bfloat16 [2, 768, 768], P('half', 'mp'), may hold values from -0.875 to 0.875
- up_weight: bfloat16 [2, 768, 3072], P('half', None, 'mp'), may hold values from -0.21875 to 0.21875
- down_weight: bfloat16 [2, 3072, 768], P('half', 'mp'), may hold values from -0.109375 to 0.109375
- norm_gains: float32 [2, 2, 768], P('half'), may hold values from 0.1 to 1.9
- cross_gain: float32 [768], replicated, may hold values from 0.1 to 1.9
- cross_query_matrix: bfloat16 [768, 768], P(None, 'mp'), may hold values from -0.21875 to 0.21875
- cross_keyval: bfloat16 [768, 2, 768], P(None, None, 'mp'), may hold values from -0.21875 to 0.21875
- cross_out: bfloat16 [768, 768], P('mp'), may hold values from -0.875 to 0.875
- slot_image: int32 [144], replicated, may hold values from 0 to 15, as said below
- slot_length: int32 [144], replicated, may hold values from 0 to 64, as said below
- cotangent: bfloat16 [2, 9216, 768], P('half', 'dp'), may hold values from -6 to 6
Outputs:
- layer_out: bfloat16 [2, 9216, 768], P('half', 'dp')
- grad_tokens: float32 [2, 9216, 768], P('half', 'dp')
- grad_qkv: float32 [2, 768, 3, 768], P('half', 'dp', None, 'mp')
- grad_out: float32 [2, 768, 768], P('half', 'mp', 'dp')
- grad_up: float32 [2, 768, 3072], P('half', 'dp', 'mp')
- grad_down: float32 [2, 3072, 768], P('half', 'mp', 'dp')
- grad_gains: float32 [2, 2, 768], P('half', None, 'dp')
- grad_cross_gain: float32 [768], P('dp')
- grad_cross_query: float32 [768, 768], P('dp', 'mp')
- grad_cross_keyval: float32 [768, 2, 768], P('dp', None, 'mp')
- grad_cross_out: float32 [768, 768], P('mp', 'dp')
Inputs may be any that keep to these rules, and one draw needn't show every extreme that they name: `slot_image`: entry k * 18 + s names the image of the caption in slot s of dp index k of the caption tower, 0 in empty slots. Images i * 2 to i * 2 + 1 are those of dp index i of the image tower. Every image is named by exactly 8 filled slots; every caption dp index k has exactly 16 filled slots, all naming images of image dp indices (k - o) modulo the number of dp indices for o from 0 to 3, at most 6 of them for each o, and that most is reached in every draw. `slot_length`: 0 exactly in empty slots, 1 or more in filled ones; every caption dp index has a caption of 64 tokens.
All inputs are finite; a program needn't handle non-finite values.
Results may differ from a plain program's by a relative error of at most 0.015.
The roundings to bfloat16 on the way count: a program that leaves them out, or rounds other values in their place, can miss the bound.
Values may be sent and summed in bfloat16 or wider, within the bound.
A program may use at most 256 MiB of HBM per device.

v0:
```python
import jax
import jax.numpy as jnp
from jax import lax
from jax.sharding import PartitionSpec as P

HEAD = 64
PATCH = 576
SLOT = 64
SPREAD = 4
IMG_DEV = 2
QCAP = 6


EPS = 1e-06
NEG = -1e30


def shifted(block, axis, distance):
    devices = range(lax.axis_size(axis))
    route = [(i - distance, i) for i in devices if i - distance in devices]
    return lax.ppermute(block, axis, route)


def passed_along(value, axis, steps):
    count = lax.axis_size(axis)
    pairs = [(source, (source + steps) % count) for source in range(count)]
    return lax.ppermute(value, axis, pairs)


def norm_rows(inputs, gain):
    mean = jnp.mean(inputs, axis=-1, keepdims=True)
    centred = inputs - mean
    return centred * lax.rsqrt(jnp.mean(centred * centred, axis=-1, keepdims=True) + EPS) * gain


def exact_error_function_activation(inputs):
    return jax.nn.gelu(inputs, approximate=False)


def matmul(left, right):
    return jnp.dot(left, right, preferred_element_type=jnp.float32)


def matmul_left(left, right):
    return lax.dot_general(
        left, right, (((0,), (0,)), ((), ())), preferred_element_type=jnp.float32
    )


def matmul_right(left, right):
    return lax.dot_general(
        left, right, (((1,), (1,)), ((), ())), preferred_element_type=jnp.float32
    )


def caption_keep(lengths, decoder_side):
    groups = lengths.shape[0]
    where_row = jnp.arange(PATCH) // SLOT
    position = jnp.arange(PATCH) % SLOT
    key_limit = jnp.broadcast_to(lengths[:, None], (groups, SLOT)).reshape(PATCH)
    same_caption = where_row[:, None] == where_row[None, :]
    causal = position[None, :] <= position[:, None]
    inside = (position[None, :] < key_limit[None, :]) | (position[None, :] == 0)
    return same_caption & causal & inside | (decoder_side == 0)


def attend_block(queries, key_rows, value_rows, keep_mask):
    factor = queries.shape[-1] ** (-0.5)
    scores = (
        jnp.einsum("qhe,khe->hqk", queries, key_rows, preferred_element_type=jnp.float32) * factor
    )
    scores = jnp.where(keep_mask[None], scores, NEG)
    row_max = jnp.max(scores, axis=-1, keepdims=True)
    exponent = jnp.exp(scores - row_max)
    row_total = jnp.sum(exponent, axis=-1, keepdims=True)
    probability = exponent / row_total
    output = jnp.einsum(
        "hqk,khe->qhe",
        probability.astype(jnp.bfloat16),
        value_rows,
        preferred_element_type=jnp.float32,
    )
    return (output, row_max + jnp.log(row_total))


def attend_back(queries, key_rows, value_rows, keep_mask, logsum, grad_output):
    factor = queries.shape[-1] ** (-0.5)
    scores = (
        jnp.einsum("qhe,khe->hqk", queries, key_rows, preferred_element_type=jnp.float32) * factor
    )
    scores = jnp.where(keep_mask[None], scores, NEG)
    probability = jnp.exp(scores - logsum)
    grad_value = jnp.einsum(
        "hqk,qhe->khe",
        probability.astype(jnp.bfloat16),
        grad_output,
        preferred_element_type=jnp.float32,
    )
    grad_prob = jnp.einsum(
        "qhe,khe->hqk", grad_output, value_rows, preferred_element_type=jnp.float32
    )
    inner_sum = jnp.sum(probability * grad_prob, axis=-1, keepdims=True)
    grad_scores = (probability * (grad_prob - inner_sum)).astype(jnp.bfloat16)
    grad_query = (
        jnp.einsum("hqk,khe->qhe", grad_scores, key_rows, preferred_element_type=jnp.float32)
        * factor
    )
    grad_key = (
        jnp.einsum("hqk,qhe->khe", grad_scores, queries, preferred_element_type=jnp.float32)
        * factor
    )
    return (grad_query, grad_key, grad_value)


def route_table(slot_image, slot_length, device, offset, dp_count, cap_dev):
    lengths = lax.dynamic_slice_in_dim(slot_length, device * cap_dev, cap_dev)
    owned = lax.dynamic_slice_in_dim(slot_image, device * cap_dev, cap_dev)
    distance = (device - owned // IMG_DEV) % dp_count
    chosen = (lengths > 0) & (distance == offset)
    ranking = jnp.cumsum(chosen.astype(jnp.int32)) - 1
    picked = chosen[None, :] & (ranking[None, :] == jnp.arange(QCAP)[:, None])
    local_image = jnp.sum(jnp.where(picked, (owned % IMG_DEV)[None, :], 0), axis=1)
    return (picked, local_image)


def row_total(partial_value):
    shares = lax.psum_scatter(partial_value, "mp", scatter_dimension=0, tiled=True)
    return lax.all_gather(shares, "mp", axis=0, tiled=True)


def to_images(values):
    return shifted(values, "half", -1)


def to_captions(values):
    return shifted(values, "half", 1)


def spread_out(values, offset):
    return passed_along(values, "dp", -offset)


def spread_back(values, offset):
    return passed_along(values, "dp", offset)


def shards(
    tokens,
    qkv_weight,
    out_weight,
    up_weight,
    down_weight,
    norm_gains,
    cross_gain,
    cross_query_matrix,
    cross_keyval,
    cross_out,
    slot_image,
    slot_length,
    cotangent,
):
    dp_count = lax.axis_size("dp")
    decoder_side = lax.axis_index("half")
    decoder_gate = decoder_side.astype(jnp.float32)
    my_index = lax.axis_index("dp")
    tok_rows = tokens[0]
    row_count, model_width = tok_rows.shape
    blocks = row_count // PATCH
    groups = PATCH // SLOT
    cap_dev = row_count // SLOT
    local_width = cross_keyval.shape[2]
    head_count = local_width // HEAD
    keyval_flat = cross_keyval.reshape(model_width, 2 * local_width)
    my_lengths = lax.dynamic_slice_in_dim(slot_length, my_index * cap_dev, cap_dev)

    def block_keep(lengths):
        return caption_keep(lengths, decoder_side)

    keep_all = jax.vmap(block_keep)(my_lengths.reshape(blocks, groups))
    full_qkv = qkv_weight[0]
    proj_out = out_weight[0]
    proj_up = up_weight[0]
    proj_down = down_weight[0]
    my_cotangent = cotangent[0]
    work_width = full_qkv.shape[2]
    work_heads = work_width // HEAD
    proj_qkv = full_qkv.reshape(model_width, 3 * work_width)
    residual = tok_rows.astype(jnp.float32)
    normed = norm_rows(residual, norm_gains[0, 0]).astype(jnp.bfloat16)
    qkv_rows = (
        matmul(normed, proj_qkv).astype(jnp.bfloat16).reshape(blocks, PATCH, 3, work_heads, HEAD)
    )

    def self_forward(member):
        block_qkv, keep_mask = member
        return attend_block(block_qkv[:, 0], block_qkv[:, 1], block_qkv[:, 2], keep_mask)

    attended, self_lse = lax.map(self_forward, (qkv_rows, keep_all))
    attended = attended.astype(jnp.bfloat16).reshape(row_count, work_width)
    hidden = residual + row_total(matmul(attended, proj_out))
    cross_in = norm_rows(hidden, cross_gain).astype(jnp.bfloat16)
    query_work = matmul(cross_in, cross_query_matrix).astype(jnp.bfloat16)
    cross_attention_rows = query_work.reshape(cap_dev, SLOT, local_width)
    image_kv = (
        matmul(tok_rows, keyval_flat)
        .astype(jnp.bfloat16)
        .reshape(blocks, PATCH, 2, head_count, HEAD)
    )
    open_mask = jnp.ones((SLOT, PATCH), bool)
    send_picks = []
    for offset in range(SPREAD):
        picked, unused = route_table(slot_image, slot_length, my_index, offset, dp_count, cap_dev)
        send_picks.append(picked.astype(jnp.bfloat16))
    selected_rows = jnp.stack(send_picks)
    packs = jnp.einsum(
        "zmf,fuh->zmuh", selected_rows, cross_attention_rows, preferred_element_type=jnp.float32
    ).astype(jnp.bfloat16)
    crossed = to_images(packs)
    served = []
    kept_items = []
    for offset in range(SPREAD):
        if offset > 0:
            arrived = spread_out(crossed[offset], offset)
        else:
            arrived = crossed[0]
        unused, local_image = route_table(
            slot_image, slot_length, (my_index + offset) % dp_count, offset, dp_count, cap_dev
        )
        item_kv = jnp.take(image_kv, local_image, axis=0)
        item_query = arrived.reshape(QCAP, SLOT, head_count, HEAD)
        item_out, item_lse = jax.vmap(attend_block, in_axes=(0, 0, 0, None))(
            item_query, item_kv[:, :, 0], item_kv[:, :, 1], open_mask
        )
        item_ctx = item_out.astype(jnp.bfloat16).reshape(QCAP, SLOT, local_width)
        if offset > 0:
            item_ctx = spread_back(item_ctx, offset)
        served.append(item_ctx)
        kept_items.append((item_query, local_image, item_lse))
    sent_home = to_captions(jnp.stack(served))
    attention_context = jnp.einsum(
        "kqh,kqyf->hyf", selected_rows, sent_home, preferred_element_type=jnp.float32
    )
    ctx_work = attention_context.astype(jnp.bfloat16).reshape(row_count, local_width)
    mixed = hidden + decoder_gate * row_total(matmul(ctx_work, cross_out))
    ffn_in = norm_rows(mixed, norm_gains[0, 1]).astype(jnp.bfloat16)
    upward = matmul(ffn_in, proj_up)
    active = exact_error_function_activation(upward).astype(jnp.bfloat16)
    result = mixed + row_total(matmul(active, proj_down))
    grad_res = my_cotangent.astype(jnp.float32)
    grad_res_low = grad_res.astype(jnp.bfloat16)
    grad_down = matmul_left(active, grad_res_low)
    grad_active = matmul_right(grad_res_low, proj_down)
    unused, gelu_pull = jax.vjp(exact_error_function_activation, upward)
    grad_upward = gelu_pull(grad_active)[0].astype(jnp.bfloat16)
    grad_up = matmul_left(ffn_in, grad_upward)
    grad_ffn_in = row_total(matmul_right(grad_upward, proj_up))
    unused, ffn_pull = jax.vjp(norm_rows, mixed, norm_gains[0, 1])
    back_mixed, grad_gain_ffn = ffn_pull(grad_ffn_in)
    grad_mixed = grad_res + back_mixed
    grad_branch = (grad_mixed * decoder_gate).astype(jnp.bfloat16)
    grad_cross_out = matmul_left(ctx_work, grad_branch)
    grad_attention_context = (
        matmul_right(grad_branch, cross_out)
        .astype(jnp.bfloat16)
        .reshape(cap_dev, SLOT, local_width)
    )
    grad_packs = jnp.einsum(
        "zmf,fuh->zmuh", selected_rows, grad_attention_context, preferred_element_type=jnp.float32
    ).astype(jnp.bfloat16)
    grad_crossed = to_images(grad_packs)
    grad_kv = jnp.zeros((blocks, PATCH, 2, head_count, HEAD), jnp.float32)
    answers = []
    for offset in range(SPREAD):
        if offset > 0:
            grad_arrived = spread_out(grad_crossed[offset], offset)
        else:
            grad_arrived = grad_crossed[0]
        item_query, local_image, item_lse = kept_items[offset]
        item_kv = jnp.take(image_kv, local_image, axis=0)
        grad_query, grad_key, grad_value = jax.vmap(attend_back, in_axes=(0, 0, 0, None, 0, 0))(
            item_query,
            item_kv[:, :, 0],
            item_kv[:, :, 1],
            open_mask,
            item_lse,
            grad_arrived.reshape(QCAP, SLOT, head_count, HEAD),
        )
        matches = (local_image[:, None] == jnp.arange(blocks)[None, :]).astype(jnp.float32)
        grad_kv = grad_kv + jnp.einsum(
            "ci,cpkhe->ipkhe",
            matches,
            jnp.stack([grad_key, grad_value], axis=2),
            precision=lax.Precision.HIGHEST,
        )
        answer = grad_query.astype(jnp.bfloat16).reshape(QCAP, SLOT, local_width)
        if offset > 0:
            answer = spread_back(answer, offset)
        answers.append(answer)
    grad_sent_home = to_captions(jnp.stack(answers))
    grad_cross_rows = jnp.einsum(
        "kqh,kqyf->hyf", selected_rows, grad_sent_home, preferred_element_type=jnp.float32
    )
    grad_query_work = grad_cross_rows.astype(jnp.bfloat16).reshape(row_count, local_width)
    grad_cross_query = matmul_left(cross_in, grad_query_work)
    grad_cross_in = row_total(matmul_right(grad_query_work, cross_query_matrix))
    unused, cross_pull = jax.vjp(norm_rows, hidden, cross_gain)
    back_hidden, grad_cross_gain = cross_pull(grad_cross_in)
    grad_hidden = grad_mixed + back_hidden
    grad_kv_low = grad_kv.astype(jnp.bfloat16).reshape(row_count, 2 * local_width)
    grad_cross_keyval = matmul_left(tok_rows, grad_kv_low).reshape(model_width, 2, local_width)
    image_part = matmul_right(grad_kv_low, keyval_flat)
    grad_hidden_low = grad_hidden.astype(jnp.bfloat16)
    grad_out = matmul_left(attended, grad_hidden_low)
    grad_attended = (
        matmul_right(grad_hidden_low, proj_out)
        .astype(jnp.bfloat16)
        .reshape(blocks, PATCH, work_heads, HEAD)
    )

    def self_backward(member):
        block_qkv, keep_mask, logsum, grad_block = member
        grad_query, grad_key, grad_value = attend_back(
            block_qkv[:, 0], block_qkv[:, 1], block_qkv[:, 2], keep_mask, logsum, grad_block
        )
        return jnp.stack([grad_query, grad_key, grad_value], axis=1).astype(jnp.bfloat16)

    grad_qkv_rows = lax.map(self_backward, (qkv_rows, keep_all, self_lse, grad_attended)).reshape(
        row_count, 3 * work_width
    )
    grad_qkv = matmul_left(normed, grad_qkv_rows).reshape(model_width, 3, work_width)
    grad_normed, image_total = row_total((matmul_right(grad_qkv_rows, proj_qkv), image_part))
    unused, first_pull = jax.vjp(norm_rows, residual, norm_gains[0, 0])
    back_source, grad_gain_attn = first_pull(grad_normed)
    grad_rows = grad_hidden + back_source + image_total
    gain_rows = jnp.stack([grad_gain_attn, grad_gain_ffn, grad_cross_gain])
    layer_out = result.astype(jnp.bfloat16)[None]
    grad_tokens = grad_rows[None]
    (
        sum_qkv,
        sum_out,
        sum_up,
        sum_down,
        sum_gain_attn,
        sum_gain_ffn,
        sum_cross_query,
        sum_cross_keyval,
        sum_cross_out,
        sum_cross_gain,
    ) = (
        lax.psum_scatter(grad_qkv, "dp", scatter_dimension=0, tiled=True),
        lax.psum_scatter(grad_out, "dp", scatter_dimension=1, tiled=True),
        lax.psum_scatter(grad_up, "dp", scatter_dimension=0, tiled=True),
        lax.psum_scatter(grad_down, "dp", scatter_dimension=1, tiled=True),
        lax.psum_scatter(gain_rows[0], "dp", scatter_dimension=0, tiled=True),
        lax.psum_scatter(gain_rows[1], "dp", scatter_dimension=0, tiled=True),
        lax.psum_scatter(grad_cross_query, "dp", scatter_dimension=0, tiled=True),
        lax.psum_scatter(grad_cross_keyval, "dp", scatter_dimension=0, tiled=True),
        lax.psum_scatter(grad_cross_out, "dp", scatter_dimension=1, tiled=True),
        lax.psum_scatter(gain_rows[2], "dp", scatter_dimension=0, tiled=True),
    )
    sum_cross_query, sum_cross_keyval, sum_cross_out, sum_cross_gain = (
        lax.psum(sum_cross_query.astype(jnp.bfloat16), "half").astype(jnp.float32),
        lax.psum(sum_cross_keyval.astype(jnp.bfloat16), "half").astype(jnp.float32),
        lax.psum(sum_cross_out.astype(jnp.bfloat16), "half").astype(jnp.float32),
        lax.psum(sum_cross_gain.astype(jnp.bfloat16), "half").astype(jnp.float32),
    )
    grad_gains = jnp.stack([sum_gain_attn, sum_gain_ffn])[None]
    return (
        layer_out,
        grad_tokens,
        sum_qkv[None],
        sum_out[None],
        sum_up[None],
        sum_down[None],
        grad_gains,
        sum_cross_gain,
        sum_cross_query,
        sum_cross_keyval,
        sum_cross_out,
    )


def solution(mesh):
    placed = (
        P("half", "dp", None),
        P("half", None, None, "mp"),
        P("half", "mp", None),
        P("half", None, "mp"),
        P("half", "mp", None),
        P("half", None, None),
        P(),
        P(None, "mp"),
        P(None, None, "mp"),
        P("mp", None),
        P(),
        P(),
        P("half", "dp", None),
    )
    return jax.shard_map(
        shards,
        mesh=mesh,
        in_specs=placed,
        out_specs=(
            P("half", "dp", None),
            P("half", "dp", None),
            P("half", "dp", None, "mp"),
            P("half", "mp", "dp"),
            P("half", "dp", "mp"),
            P("half", "mp", "dp"),
            P("half", None, "dp"),
            P("dp"),
            P("dp", "mp"),
            P("dp", None, "mp"),
            P("mp", "dp"),
        ),
        check_vma=False,
    )
```

profile of v0, /device:TPU:4, one launch (start us, length us, event | category | flops | bytes accessed | tf_op | source)
XLA Modules:
  0.0 1443.7 jit_solution(12112006343673895061)
XLA Ops:
  41.5 29.6 %while.22 = (s32[]{:T(128)}, bf16[2,576,6,64]{1,3,2,0:T(8,128)(2,1)}, f32[2,6,576,1]{2,1,3,0:T(8,128)S(1)}, bf16[2,576,3,6,64]{1,4,3,2,0:T(8,128)(2,1)}, pred[2,576,576]{1,2,0:T(8,128)(4,1)S(1)}, /*index=5*/s32[]{:T(128)}) while((s32[]{:T(128)}, bf16[2,576,6,64]{1,3,2,0:T(8,128)(2,1)}, f32[2,6,576,1]{2,1,3,0:T(8,128)S(1)}, ...), condition=%wide.region_5.6_spmd, body=%wide.region_2.5_spmd.sunk | while | flops 533492352 | bytes 38740628 | solution.py:198
  188.4 8.6 collective-permute-done.1
  237.8 9.7 collective-permute-done.6
  250.1 28.7 %collective-permute-done.7 = bf16[4,6,64,384]{3,2,1,0:T(8,128)(2,1)S(1)} collective-permute-done((bf16[4,6,64,384]{3,2,1,0:T(8,128)(2,1)S(1)}, bf16[4,6,64,384]{3,2,1,0:T(8,128)(2,1)S(1)}, u32[]{:S(2)}, u32[]{:S(2)}) %collective-permute-start.7) | collective-permute-done | bytes 1179680 | tf_op jit(solution)/shard_map/ppermute | solution.py:21
  284.2 9.0 reduce-scatter.16.cloned.1.call-done
  293.3 15.2 %all-gather.10.cloned.1.call-done = f32[1152,768]{1,0:T(8,128)} async-done(((f32[576,768]{1,0:T(8,128)}), f32[1152,768]{1,0:T(8,128)}) %all-gather.10.cloned.1.call-update) | async-done | bytes 3538960 | tf_op jit(solution)/shard_map/all_gather | solution.py:128
  312.7 19.1 %multiply_convert_fusion.1 = (bf16[1152,1536]{1,0:T(8,128)(2,1)}, f32[1152,1536]{1,0:T(8,128)S(1)}, f32[1152,1536]{1,0:T(8,128)}) fusion(bf16[1,768,1536]{2,1,0:T(8,128)(2,1)S(1)} %copy-done, f32[1152,768]{1,0:T(8,128)S(1)} %get-tuple-element.163, f32[768]{0:T(1024)S(1)} %copy-done.73, f32[1152]{0:T(1024)S(1)} %fusion.162, f32[1152]{0:T(1024)S(1)} %broadcast_multiply_fusion), kind=kOutput, calls=%fused_computation.68 | convolution fusion | flops 2836463616 | bytes 23605248 | tf_op jit(solution)/shard_map/dot_general | solution.py:41
  358.0 14.7 %reduce-scatter.18.cloned.1.call-done = f32[576,768]{1,0:T(8,128)} async-done(((f32[1152,768]{1,0:T(8,128)}), f32[576,768]{1,0:T(8,128)}) %reduce-scatter.18.cloned.1.call-update) | async-done | bytes 1769488 | tf_op jit(solution)/shard_map/reduce_scatter | solution.py:127
  372.8 15.4 %all-gather.14.cloned.1.call-done = f32[1152,768]{1,0:T(8,128)} async-done(((f32[576,768]{1,0:T(8,128)}), f32[1152,768]{1,0:T(8,128)}) %all-gather.14.cloned.1.call-update) | async-done | bytes 3538960 | tf_op jit(solution)/shard_map/all_gather | solution.py:128
  392.9 10.7 all-gather.12.cloned.1.call-done
  416.6 25.3 %collective-permute-done.8 = bf16[4,6,64,384]{3,2,1,0:T(8,128)(2,1)S(1)} collective-permute-done((bf16[4,6,64,384]{3,2,1,0:T(8,128)(2,1)S(1)}, bf16[4,6,64,384]{3,2,1,0:T(8,128)(2,1)S(1)}, u32[]{:S(2)}, u32[]{:S(2)}) %collective-permute-start.8) | collective-permute-done | bytes 1179680 | tf_op jit(solution)/shard_map/ppermute | solution.py:21
  515.7 11.4 collective-permute-done.14
  528.6 28.6 %collective-permute-done.15 = bf16[4,6,64,384]{3,2,1,0:T(8,128)(2,1)S(1)} collective-permute-done((bf16[4,6,64,384]{3,2,1,0:T(8,128)(2,1)S(1)}, bf16[4,6,64,384]{3,2,1,0:T(8,128)(2,1)S(1)}, u32[]{:S(2)}, u32[]{:S(2)}) %collective-permute-start.15) | collective-permute-done | bytes 1179680 | tf_op jit(solution)/shard_map/ppermute | solution.py:21
  561.8 9.0 reduce-scatter.22.cloned.1.call-done
  580.0 9.0 pad_maximum_fusion
  616.0 31.6 %while.23 = (s32[]{:T(128)}, bf16[2,576,3,6,64]{1,4,3,2,0:T(8,128)(2,1)}, bf16[2,576,3,6,64]{1,4,3,2,0:T(8,128)(2,1)}, pred[2,576,576]{1,2,0:T(8,128)(4,1)S(1)},...) while((s32[]{:T(128)}, bf16[2,576,3,6,64]{1,4,3,2,0:T(8,128)(2,1)}, ...), condition=%wide.region_45.47_spmd, body=%wide.region_43.46_spmd.sunk | while | flops 1308963456 | bytes 99360440 | solution.py:327
  685.1 8.2 pad_maximum_fusion.1
  693.2 10.4 pad_maximum_fusion.2
  703.6 8.0 pad_maximum_fusion.3
  711.7 20.1 %fusion.36 = f32[2,576,2,6,64]{1,0,4,3,2:T(2,128)} fusion(f32[6,576,2,6,64]{1,4,3,0,2:T(8,128)} %pad_maximum_fusion.1, s32[6]{0:T(128)S(1)} %copy-done.117), kind=kOutput, calls=%fused_computation.56 | convolution fusion | flops 63701004 | bytes 14155800 | tf_op jit(solution)/shard_map/ci,cpkhe->ipkhe/dot_general | solution.py:289
  731.8 15.2 %fusion.34 = f32[2,576,2,6,64]{1,0,4,3,2:T(2,128)} fusion(f32[6,576,2,6,64]{1,4,3,0,2:T(8,128)S(1)} %copy-done.10, s32[6]{0:T(128)S(1)} %copy-done.115), kind=kOutput, calls=%fused_computation.54 | convolution fusion | flops 63701004 | bytes 14155800 | tf_op jit(solution)/shard_map/ci,cpkhe->ipkhe/dot_general | solution.py:289
  746.9 20.2 %fusion.32 = f32[2,576,2,6,64]{1,0,4,3,2:T(2,128)} fusion(f32[6,576,2,6,64]{1,4,3,0,2:T(8,128)} %pad_maximum_fusion.3, s32[6]{0:T(128)S(1)} %copy-done.113), kind=kOutput, calls=%fused_computation.52 | convolution fusion | flops 63701004 | bytes 14155800 | tf_op jit(solution)/shard_map/ci,cpkhe->ipkhe/dot_general | solution.py:289
  767.2 19.4 %add_convert_fusion.1 = bf16[2,576,2,6,64]{1,0,4,3,2:T(2,128)(2,1)S(1)} fusion(f32[2,576,2,6,64]{1,0,4,3,2:T(2,128)} %fusion.32, f32[2,576,2,6,64]{1,0,4,3,2:T(2,128)} %fusion.34, f32[2,576,2,6,64]{1,0,4,3,2:T(2,128)} %fusion.36, f32[6,576,2,6,64]{1,4,3,0,2:T(8,128)S(1)} %bitcast.482, s32[6]{0:T(128)S(1)} %copy-done.124), kind=kOutput, calls=%fused_computation.128 | convolution fusion | flops 67239952 | bytes 23003160 | tf_op jit(solution)/shard_map/ci,cpkhe->ipkhe/dot_general | solution.py:289
  817.9 57.4 %reduce-scatter.38.cloned.1.call-done = f32[384,96]{0,1:T(8,128)} async-done(((f32[384,768]{0,1:T(8,128)}), f32[384,96]{0,1:T(8,128)}) %reduce-scatter.38.cloned.1.call-update) | async-done | bytes 147472 | tf_op jit(solution)/shard_map/reduce_scatter | solution.py:358
  876.9 65.1 %reduce-scatter.36.cloned.1.call-done = f32[96,384]{1,0:T(8,128)} async-done(((f32[768,384]{1,0:T(8,128)}), f32[96,384]{1,0:T(8,128)}) %reduce-scatter.36.cloned.1.call-update) | async-done | bytes 147472 | tf_op jit(solution)/shard_map/reduce_scatter | solution.py:356
  943.6 11.9 all-gather.18.cloned.1.call-done
  960.3 101.0 %all-reduce.10 = (f32[768]{0:T(1024)S(1)}, f32[768]{0:T(1024)S(1)}, bf16[768]{0:T(1024)(128)(2,1)S(1)}, bf16[768,2,384]{2,1,0:T(2,128)(2,1)}) all-reduce(f32[768]{0:T(1024)S(1)} %copy-done.109, f32[768]{0:T(1024)S(1)} %get-tuple-element.123, f32[768]{0:T(1024)S(1)} %copy-done.110, ...), channel_id=14, replica_groups=mesh['half'=2,'dp'=8,'mp'=2] {'dp'}, use_global_device_ids=true, to_apply=%region_57.59.clone | all-reduce | flops 592128 | bytes 3555840
  1063.0 8.7 fusion.204
  1110.3 75.8 %reduce-scatter.32.cloned.1.call-done = f32[96,1536]{1,0:T(8,128)} async-done(((f32[768,1536]{1,0:T(8,128)}), f32[96,1536]{1,0:T(8,128)}) %reduce-scatter.32.cloned.1.call-update) | async-done | bytes 589840 | tf_op jit(solution)/shard_map/reduce_scatter | solution.py:352
  1186.1 99.7 %reduce-scatter.34.cloned.1.call-done = f32[1536,96]{0,1:T(8,128)} async-done(((f32[1536,768]{0,1:T(8,128)}), f32[1536,96]{0,1:T(8,128)}) %reduce-scatter.34.cloned.1.call-update) | async-done | bytes 589840 | tf_op jit(solution)/shard_map/reduce_scatter | solution.py:353
  1285.8 68.0 %reduce-scatter.30.cloned.1.call-done = f32[384,96]{0,1:T(8,128)} async-done(((f32[384,768]{0,1:T(8,128)}), f32[384,96]{0,1:T(8,128)}) %reduce-scatter.30.cloned.1.call-update) | async-done | bytes 147472 | tf_op jit(solution)/shard_map/reduce_scatter | solution.py:351
  1353.9 82.8 %reduce-scatter.28.cloned.1.call-done = f32[96,3,384]{2,0,1:T(8,128)} async-done(((f32[768,3,384]{2,0,1:T(8,128)}), f32[96,3,384]{2,0,1:T(8,128)}) %reduce-scatter.28.cloned.1.call-update) | async-done | bytes 442384 | tf_op jit(solution)/shard_map/reduce_scatter | solution.py:350
  (635 shorter events, 527.5 us)
Async XLA Ops:
  7.2 93.9 %reduce-scatter.14.cloned.1.call-start = ((), (), s32[]{:S(2)}) async-start(), calls=%async_computation.13 | async-start | bytes 5308416 | tf_op jit(solution)/shard_map/reduce_scatter | solution.py:127
  82.0 55.5 %all-gather.8.cloned.1.call-start = ((), (), s32[]{:S(2)}) async-start(), calls=%async_computation.14 | async-start | bytes 5308416 | tf_op jit(solution)/shard_map/all_gather | solution.py:128
  101.1 192.1 %reduce-scatter.16.cloned.1.call-start = ((), (), s32[]{:S(2)}) async-start(), calls=%async_computation.15 | async-start | bytes 5308416 | tf_op jit(solution)/shard_map/reduce_scatter | solution.py:127
  145.1 26.9 %collective-permute-start = (bf16[4,6,64,384]{3,2,1,0:T(8,128)(2,1)S(1)}, bf16[4,6,64,384]{3,2,1,0:T(8,128)(2,1)}, u32[]{:S(2)}, u32[]{:S(2)}) collective-permute-start(bf16[4,6,64,384]{3,2,1,0:T(8,128)(2,1)S(1)} %copy.226), channel_id=1, source_target_pairs={{16,0},{17,1},{18,2},{19,3},{20,4},{21,5},{22,6},{23,7},{24,8},{25... | collective-permute-start | bytes 3538952 | tf_op jit(solution)/shard_map/ppermute | solution.py:21
  174.5 49.6 %collective-permute-start.5 = (bf16[6,64,384]{2,1,0:T(8,128)(2,1)S(1)}, bf16[6,64,384]{2,1,0:T(8,128)(2,1)S(1)}, u32[]{:S(2)}, u32[]{:S(2)}) collective-permute-start(bf16[6,64,384]{2,1,0:T(8,128)(2,1)S(1)} %get-tuple-element.194), channel_id=1, source_target_pairs={{0,10},{2,12},{4,14},{6,0},{8,2},{10,4},{12,6},{14,8},{1,11},{3,13... | collective-permute-start | bytes 884744 | tf_op jit(solution)/shard_map/ppermute | solution.py:27
  178.7 29.8 %collective-permute-start.3 = (bf16[6,64,384]{2,1,0:T(8,128)(2,1)}, bf16[6,64,384]{2,1,0:T(8,128)(2,1)}, u32[]{:S(2)}, u32[]{:S(2)}) collective-permute-start(bf16[6,64,384]{2,1,0:T(8,128)(2,1)} %get-tuple-element.195), channel_id=1, source_target_pairs={{0,12},{2,14},{4,0},{6,2},{8,4},{10,6},{12,8},{14,10},{1,13},{3,15... | collective-permute-start | bytes 884744 | tf_op jit(solution)/shard_map/ppermute | solution.py:27
  206.0 31.8 %collective-permute-start.2 = (bf16[6,64,384]{2,1,0:T(8,128)(2,1)}, bf16[6,64,384]{2,1,0:T(8,128)(2,1)}, u32[]{:S(2)}, u32[]{:S(2)}) collective-permute-start(bf16[6,64,384]{2,1,0:T(8,128)(2,1)} %copy.232), channel_id=1, source_target_pairs={{0,2},{2,4},{4,6},{6,8},{8,10},{10,12},{12,14},{14,0},{1,3},{3,5},... | collective-permute-start | bytes 884744 | tf_op jit(solution)/shard_map/ppermute | solution.py:27
  248.8 30.0 %collective-permute-start.7 = (bf16[4,6,64,384]{3,2,1,0:T(8,128)(2,1)S(1)}, bf16[4,6,64,384]{3,2,1,0:T(8,128)(2,1)S(1)}, u32[]{:S(2)}, u32[]{:S(2)}) collective-permute-start(bf16[4,6,64,384]{3,2,1,0:T(8,128)(2,1)S(1)} %pad_maximum_fusion.4), channel_id=1, source_target_pairs={{0,16},{1,17},{2,18},{3,19},{4,20},{5,21},{6,22},{7,23},{8,24},{9,... | collective-permute-start | bytes 3538952 | tf_op jit(solution)/shard_map/ppermute | solution.py:21
  284.2 24.3 %all-gather.10.cloned.1.call-start = ((), (), s32[]{:S(2)}) async-start(), calls=%async_computation.16 | async-start | bytes 5308416 | tf_op jit(solution)/shard_map/all_gather | solution.py:128
  293.2 64.7 %reduce-scatter.20.cloned.1.call-start = ((), (), s32[]{:S(2)}) async-start(), calls=%async_computation.19 | async-start | bytes 5308416 | tf_op jit(solution)/shard_map/reduce_scatter | solution.py:127
  345.3 27.5 %reduce-scatter.18.cloned.1.call-start = ((), (), s32[]{:S(2)}) async-start(), calls=%async_computation.17 | async-start | bytes 5308416 | tf_op jit(solution)/shard_map/reduce_scatter | solution.py:127
  354.0 34.1 %all-gather.14.cloned.1.call-start = ((), (), s32[]{:S(2)}) async-start(), calls=%async_computation.20 | async-start | bytes 5308416 | tf_op jit(solution)/shard_map/all_gather | solution.py:128
  358.0 45.7 %all-gather.12.cloned.1.call-start = ((), (), s32[]{:S(2)}) async-start(), calls=%async_computation.18 | async-start | bytes 5308416 | tf_op jit(solution)/shard_map/all_gather | solution.py:128
  372.8 198.0 %reduce-scatter.22.cloned.1.call-start = ((), (), s32[]{:S(2)}) async-start(), calls=%async_computation.21 | async-start | bytes 5308416 | tf_op jit(solution)/shard_map/reduce_scatter | solution.py:127
  414.2 27.8 %collective-permute-start.8 = (bf16[4,6,64,384]{3,2,1,0:T(8,128)(2,1)S(1)}, bf16[4,6,64,384]{3,2,1,0:T(8,128)(2,1)S(1)}, u32[]{:S(2)}, u32[]{:S(2)}) collective-permute-start(bf16[4,6,64,384]{3,2,1,0:T(8,128)(2,1)S(1)} %copy.247), channel_id=1, source_target_pairs={{16,0},{17,1},{18,2},{19,3},{20,4},{21,5},{22,6},{23,7},{24,8},{25... | collective-permute-start | bytes 3538952 | tf_op jit(solution)/shard_map/ppermute | solution.py:21
  442.4 56.3 %collective-permute-start.13 = (bf16[6,64,384]{2,1,0:T(8,128)(2,1)S(1)}, bf16[6,64,384]{2,1,0:T(8,128)(2,1)S(1)}, u32[]{:S(2)}, u32[]{:S(2)}) collective-permute-start(bf16[6,64,384]{2,1,0:T(8,128)(2,1)S(1)} %get-tuple-element.190), channel_id=1, source_target_pairs={{0,10},{2,12},{4,14},{6,0},{8,2},{10,4},{12,6},{14,8},{1,11},{3,13... | collective-permute-start | bytes 884744 | tf_op jit(solution)/shard_map/ppermute | solution.py:27
  446.1 33.5 %collective-permute-start.11 = (bf16[6,64,384]{2,1,0:T(8,128)(2,1)S(1)}, bf16[6,64,384]{2,1,0:T(8,128)(2,1)S(1)}, u32[]{:S(2)}, u32[]{:S(2)}) collective-permute-start(bf16[6,64,384]{2,1,0:T(8,128)(2,1)S(1)} %get-tuple-element.191), channel_id=1, source_target_pairs={{0,12},{2,14},{4,0},{6,2},{8,4},{10,6},{12,8},{14,10},{1,13},{3,15... | collective-permute-start | bytes 884744 | tf_op jit(solution)/shard_map/ppermute | solution.py:27
  476.9 38.8 %collective-permute-start.10 = (bf16[6,64,384]{2,1,0:T(8,128)(2,1)S(1)}, bf16[6,64,384]{2,1,0:T(8,128)(2,1)S(1)}, u32[]{:S(2)}, u32[]{:S(2)}) collective-permute-start(bf16[6,64,384]{2,1,0:T(8,128)(2,1)S(1)} %copy.250), channel_id=1, source_target_pairs={{0,2},{2,4},{4,6},{6,8},{8,10},{10,12},{12,14},{14,0},{1,3},{3,5},... | collective-permute-start | bytes 884744 | tf_op jit(solution)/shard_map/ppermute | solution.py:27
  491.8 23.9 %collective-permute-start.12 = (bf16[6,64,384]{2,1,0:T(8,128)(2,1)S(1)}, bf16[6,64,384]{2,1,0:T(8,128)(2,1)S(1)}, u32[]{:S(2)}, u32[]{:S(2)}) collective-permute-start(bf16[6,64,384]{2,1,0:T(8,128)(2,1)S(1)} %copy.252), channel_id=1, source_target_pairs={{0,4},{2,6},{4,8},{6,10},{8,12},{10,14},{12,0},{14,2},{1,5},{3,7},... | collective-permute-start | bytes 884744 | tf_op jit(solution)/shard_map/ppermute | solution.py:27
  527.3 29.9 %collective-permute-start.15 = (bf16[4,6,64,384]{3,2,1,0:T(8,128)(2,1)S(1)}, bf16[4,6,64,384]{3,2,1,0:T(8,128)(2,1)S(1)}, u32[]{:S(2)}, u32[]{:S(2)}) collective-permute-start(bf16[4,6,64,384]{3,2,1,0:T(8,128)(2,1)S(1)} %pad_maximum_fusion.5), channel_id=1, source_target_pairs={{0,16},{1,17},{2,18},{3,19},{4,20},{5,21},{6,22},{7,23},{8,24},{9,... | collective-permute-start | bytes 3538952 | tf_op jit(solution)/shard_map/ppermute | solution.py:21
  561.7 39.6 %all-gather.16.cloned.1.call-start = ((), (), s32[]{:S(2)}) async-start(), calls=%async_computation.22 | async-start | bytes 5308416 | tf_op jit(solution)/shard_map/all_gather | solution.py:128
  570.7 232.4 %reduce-scatter.24.cloned.1.call-start = ((), (), s32[]{:S(2)}) async-start(), calls=%async_computation.23 | async-start | bytes 5308416 | tf_op jit(solution)/shard_map/reduce_scatter | solution.py:127
  667.1 139.6 %reduce-scatter.26.cloned.1.call-start = ((), (), s32[]{:S(2)}) async-start(), calls=%async_computation.25 | async-start | bytes 5308416 | tf_op jit(solution)/shard_map/reduce_scatter | solution.py:127
  794.0 81.3 %reduce-scatter.38.cloned.1.call-start = ((), (), s32[]{:S(2)}) async-start(), calls=%async_computation.32 | async-start | bytes 1327104 | tf_op jit(solution)/shard_map/reduce_scatter | solution.py:358
  798.9 143.2 %reduce-scatter.36.cloned.1.call-start = ((), (), s32[]{:S(2)}) async-start(), calls=%async_computation.31 | async-start | bytes 1327104 | tf_op jit(solution)/shard_map/reduce_scatter | solution.py:356
  803.1 152.5 %all-gather.18.cloned.1.call-start = ((), (), s32[]{:S(2)}) async-start(), calls=%async_computation.24 | async-start | bytes 5308416 | tf_op jit(solution)/shard_map/all_gather | solution.py:128
  803.7 294.9 %all-gather.20.cloned.1.call-start = ((), (), s32[]{:S(2)}) async-start(), calls=%async_computation.26 | async-start | bytes 5308416 | tf_op jit(solution)/shard_map/all_gather | solution.py:128
  806.7 298.7 %all-reduce.9.cloned.1.call-start = ((), (), s32[]{:S(2)}) async-start(), calls=%async_computation.33 | async-start | bytes 589824 | tf_op jit(solution)/shard_map/psum | solution.py:362
  1062.9 123.2 %reduce-scatter.32.cloned.1.call-start = ((), (), s32[]{:S(2)}) async-start(), calls=%async_computation.29 | async-start | bytes 5308416 | tf_op jit(solution)/shard_map/reduce_scatter | solution.py:352
  1071.8 214.1 %reduce-scatter.34.cloned.1.call-start = ((), (), s32[]{:S(2)}) async-start(), calls=%async_computation.30 | async-start | bytes 5308416 | tf_op jit(solution)/shard_map/reduce_scatter | solution.py:353
  1080.0 273.8 %reduce-scatter.30.cloned.1.call-start = ((), (), s32[]{:S(2)}) async-start(), calls=%async_computation.28 | async-start | bytes 1327104 | tf_op jit(solution)/shard_map/reduce_scatter | solution.py:351
  1085.5 351.1 %reduce-scatter.28.cloned.1.call-start = ((), (), s32[]{:S(2)}) async-start(), calls=%async_computation.27 | async-start | bytes 3981312 | tf_op jit(solution)/shard_map/reduce_scatter | solution.py:350
  (161 other events, 3002.1 us)
Sparse Core Ops, SparseCore 0:
  82.1 12.8 reduce-scatter.13
  101.2 14.1 all-gather.7
  284.3 8.8 reduce-scatter.15
  294.6 13.8 all-gather.9
  345.4 12.5 reduce-scatter.19
  360.1 12.5 reduce-scatter.17
  374.3 13.8 all-gather.13
  389.7 13.8 all-gather.11
  561.8 8.8 reduce-scatter.21
  572.2 13.8 all-gather.15
  667.2 12.5 reduce-scatter.23
  794.1 12.4 reduce-scatter.25
  810.5 64.8 reduce-scatter.37
  879.0 63.0 reduce-scatter.35
  943.5 11.9 all-gather.17
  957.0 13.8 all-gather.19
  1063.1 22.0 all-reduce.8
  1089.7 96.3 reduce-scatter.31
  1190.8 95.0 reduce-scatter.33
  1290.0 63.7 reduce-scatter.29
  1358.5 78.1 reduce-scatter.27
where the time goes:
time: 1450 us; the launch traced here: 1440 us
  waiting for transfers between devices  666 us (46%)
  matrix products  321 us (22%)
  other arithmetic  145 us (10%)
  local copies, waits for them, and re-layouts  136 us (9%)
  blocking collectives  106 us (7%)
  starting transfers between devices  40.3 us (3%)
  between operations  17.5 us (1%)
    unnamed x1, blocking collectives  101 us
    reduce_scatter x1, waiting for transfers between devices, shards(): lax.psum_scatter(grad_down, 'dp', scatter_dimension=1, tiled=True)  99.7 us
    ppermute x4, waiting for transfers between devices, shifted(): return lax.ppermute(block, axis, route)  85.9 us
    reduce_scatter x1, waiting for transfers between devices, shards(): lax.psum_scatter(grad_qkv, 'dp', scatter_dimension=0, tiled=True)  82.8 us
    reduce_scatter x1, waiting for transfers between devices, shards(): lax.psum_scatter(grad_up, 'dp', scatter_dimension=0, tiled=True)  75.8 us
    dot_general x4, matrix products, shards(): jnp.einsum('ci,cpkhe->ipkhe', matches, jnp.stack([grad_key, grad_value],...  74.8 us
    reduce_scatter x1, waiting for transfers between devices, shards(): lax.psum_scatter(grad_out, 'dp', scatter_dimension=1, tiled=True)  68 us
    reduce_scatter x1, waiting for transfers between devices, shards(): lax.psum_scatter(grad_cross_query, 'dp', scatter_dimension=0, tiled=True)  65.1 us
  transfers between devices with their start and end apart: 37, of which 23 were waited for; matrix products, arithmetic and copies ran while one was open for 28% of the time, Pallas kernels for 0%

commit v1 on v0

v1 whole, which is shorter than its diff:
```python
import functools

import jax
import jax.numpy as jnp
from jax import lax
from jax.experimental import pallas as pl
from jax.experimental.pallas import tpu as pltpu
from jax.sharding import PartitionSpec as P

HEAD = 64
PATCH = 576
SLOT = 64
SPREAD = 4
IMG_DEV = 2
QCAP = 6
CAPS = 8

EPS = 1e-06
NEG = -1e30
SCALE = HEAD**-0.5

F32 = jnp.float32
BF16 = jnp.bfloat16
VMEM = pl.BlockSpec(memory_space=pltpu.VMEM)
SMEM = pl.BlockSpec(memory_space=pltpu.SMEM)
ANY = pl.BlockSpec(memory_space=pl.ANY)
LIMIT = 56 * 1024 * 1024


def dot(a, b):
    return lax.dot_general(a, b, (((1,), (0,)), ((), ())), preferred_element_type=F32)


def dot_nt(a, b):
    return lax.dot_general(a, b, (((1,), (1,)), ((), ())), preferred_element_type=F32)


def dot_tn(a, b):
    return lax.dot_general(a, b, (((0,), (0,)), ((), ())), preferred_element_type=F32)


def norm_stats(v):
    mean = jnp.mean(v, axis=-1, keepdims=True)
    centred = v - mean
    rstd = lax.rsqrt(jnp.mean(centred * centred, axis=-1, keepdims=True) + EPS)
    return centred * rstd, rstd


def norm_rows(v, gain):
    return norm_stats(v)[0] * gain


def norm_back(v, gain, dn):
    x_hat, rstd = norm_stats(v)
    dg = dn * gain
    m1 = jnp.mean(dg, axis=-1, keepdims=True)
    m2 = jnp.mean(dg * x_hat, axis=-1, keepdims=True)
    return (dg - m1 - x_hat * m2) * rstd, jnp.sum(dn * x_hat, axis=0, keepdims=True)


def head_masks():
    lane = lax.broadcasted_iota(jnp.int32, (1, 2 * HEAD), 1)
    first = (lane < HEAD).astype(F32)
    return first.astype(BF16), (1.0 - first).astype(BF16)


def three(ref, half):
    return jnp.concatenate([ref[3 * half], ref[3 * half + 1], ref[3 * half + 2]], axis=1)


def attend(q, k, v, masks, bias):
    v_t = v.T
    outs, sums = [], []
    for h in range(2):
        s = dot_nt(k, q * masks[h])
        if bias is not None:
            s = s + bias
        top = jnp.max(s, axis=0, keepdims=True)
        e = jnp.exp(s - top)
        total = jnp.sum(e, axis=0, keepdims=True)
        p = (e * (1.0 / total)).astype(BF16)
        outs.append(dot(v_t[h * HEAD : (h + 1) * HEAD], p))
        sums.append(top + jnp.log(total))
    return jnp.concatenate(outs, axis=0).T.astype(BF16), sums


def attend_back(q, k, v, do, masks, bias, sums):
    k_t = k.T
    dqs = []
    dk = dv = None
    for h in range(2):
        qh = q * masks[h]
        doh = do * masks[h]
        s = dot_nt(k, qh)
        if bias is not None:
            s = s + bias
        if sums is None:
            e = jnp.exp(s - jnp.max(s, axis=0, keepdims=True))
            p = e * (1.0 / jnp.sum(e, axis=0, keepdims=True))
        else:
            p = jnp.exp(s - sums[h])
        dp = dot_nt(v, doh)
        delta = jnp.sum(p * dp, axis=0, keepdims=True)
        ds = (p * (dp - delta)).astype(BF16)
        dv_h = dot(p.astype(BF16), doh)
        dk_h = dot(ds, qh)
        dv = dv_h if dv is None else dv + dv_h
        dk = dk_h if dk is None else dk + dk_h
        dqs.append(dot(k_t[h * HEAD : (h + 1) * HEAD], ds))
    dq = (jnp.concatenate(dqs, axis=0) * SCALE).T
    return dq.astype(BF16), dk.astype(BF16), dv.astype(BF16)


GROUP = 3 * SLOT


def caption_bias(meta, bias):
    key = lax.broadcasted_iota(jnp.int32, (GROUP, GROUP), 0)
    query = lax.broadcasted_iota(jnp.int32, (GROUP, GROUP), 1)
    key_slot, key_pos = key >> 6, key & 63
    same = (key_slot == (query >> 6)) & (key_pos <= (query & 63))
    for g in range(3):
        limit = jnp.where(
            key_slot == 0,
            meta[1 + 3 * g],
            jnp.where(key_slot == 1, meta[2 + 3 * g], meta[3 + 3 * g]),
        )
        keep = same & ((key_pos < limit) | (key_pos == 0))
        bias[g] = jnp.where(keep, 0.0, NEG)


def pre_kernel(meta, x, gain, gain_cross, w_own, w_oth, o_own, o_oth, a_ref, r_ref, n_ref, q_ref, k_ref, v_ref, t_ref, bias):
    source = x[...].astype(F32)
    normed = norm_rows(source, gain[0:1, :]).astype(BF16)
    n_ref[...] = normed

    @pl.when(meta[0] == 0)
    def _():
        a_ref[...] = normed
        r_ref[...] = source

    @pl.when(meta[0] == 1)
    def _():
        caption_bias(meta, bias)
        for half, w in ((0, w_own), (1, w_oth)):
            for j, ref in enumerate((q_ref, k_ref, v_ref)):
                rows = dot(n_ref[...], w[j]).astype(BF16)
                if j == 0:
                    rows = rows * SCALE
                for p in range(3):
                    ref[3 * half + p] = rows[:, p * 128 : (p + 1) * 128]
        masks = head_masks()

        @pl.loop(0, 6)
        def _(p):
            for g in range(3):
                at = slice(g * GROUP, (g + 1) * GROUP)
                out, unused = attend(q_ref[p, at], k_ref[p, at], v_ref[p, at], masks, bias[g])
                t_ref[p, at] = out

        hidden = x[...].astype(F32) + dot(three(t_ref, 0), o_own[...]) + dot(three(t_ref, 1), o_oth[...])
        r_ref[...] = hidden
        a_ref[...] = norm_rows(hidden, gain_cross[...]).astype(BF16)


def mid_kernel(meta, a_ref, b_ref, r_ref, gain, w_own, w_oth, o_own, o_oth, q_ref, k_ref, v_ref, c_ref, s_ref, m_ref, f_ref):
    rows_in = a_ref.shape[0]
    for half, w in ((0, w_own), (1, w_oth)):
        for j, (ref, src) in enumerate(((q_ref, a_ref), (k_ref, b_ref), (v_ref, b_ref))):
            rows = dot(src[...], w[j]).astype(BF16)
            if j == 0:
                rows = rows * SCALE
            for p in range(3):
                ref[3 * half + p] = rows[:, p * 128 : (p + 1) * 128]
    masks = head_masks()

    @pl.loop(0, 6)
    def _(p):
        out, sums = attend(q_ref[p], k_ref[p], v_ref[p], masks, None)
        c_ref[p] = out
        s_ref[2 * p] = sums[0]
        s_ref[2 * p + 1] = sums[1]

    @pl.when(meta[0] == 1)
    def _():
        for p in range(6):
            c_ref[p, CAPS * SLOT : rows_in] = jnp.zeros((rows_in - CAPS * SLOT, 128), BF16)

    mixed = r_ref[...] + dot(three(c_ref, 0), o_own[...]) + dot(three(c_ref, 1), o_oth[...])
    m_ref[...] = mixed
    f_ref[...] = norm_rows(mixed, gain[1:2, :]).astype(BF16)


def ffn_kernel(last, f_ref, cot, up, down, *rest):
    if last:
        out_in, grad_in, mixed, gain, g_ref, y_ref, gm_ref, gg_ref, acc_out, acc_grad = rest
    else:
        g_ref, acc_out, acc_grad = rest
    step = pl.program_id(0)

    @pl.when(step == 0)
    def _():
        if last:
            acc_out[...] = out_in[...]
            acc_grad[...] = grad_in[...]
        else:
            acc_out[...] = jnp.zeros_like(acc_out)
            acc_grad[...] = jnp.zeros_like(acc_grad)

    upward = dot(f_ref[...], up[...])
    phi = 0.5 * (1.0 + lax.erf(upward * (0.5**0.5)))
    active = (upward * phi).astype(BF16)
    slope = phi + upward * (jnp.exp(-0.5 * upward * upward) * 0.3989422804014327)
    grad_active = dot_nt(cot[...], down[...])
    grad_upward = (grad_active * slope).astype(BF16)
    acc_out[...] += dot(active, down[...])
    g_ref[1] = dot_tn(cot[...], active).astype(BF16)
    g_ref[0] = dot_tn(f_ref[...], grad_upward).astype(BF16)
    acc_grad[...] += dot_nt(grad_upward, up[...])
    if last:

        @pl.when(step == pl.num_programs(0) - 1)
        def _():
            y_ref[...] = (mixed[...] + acc_out[...]).astype(BF16)
            back, gain_grad = norm_back(mixed[...], gain[1:2, :], acc_grad[...])
            gm_ref[...] = cot[...].astype(F32) + back
            gg_ref[...] = gain_grad


def back_kernel(meta, gm_ref, c_ref, s_ref, q_ref, k_ref, v_ref, a_ref, b_ref, w_own, w_oth, o_own, o_oth, g_own, g_oth, da_ref, db_ref, do_ref, dq_ref, dk_ref, dv_ref):
    rows_in = a_ref.shape[0]
    low = gm_ref[...].astype(BF16)
    for half, o, g in ((0, o_own, g_own), (1, o_oth, g_oth)):
        g[0] = dot_tn(low, three(c_ref, half)).astype(BF16)
        rows = dot_nt(low, o[...]).astype(BF16)
        for p in range(3):
            do_ref[3 * half + p] = rows[:, p * 128 : (p + 1) * 128]

    @pl.when(meta[0] == 1)
    def _():
        for p in range(6):
            do_ref[p, CAPS * SLOT : rows_in] = jnp.zeros((rows_in - CAPS * SLOT, 128), BF16)

    masks = head_masks()

    @pl.loop(0, 6)
    def _(p):
        sums = (s_ref[2 * p], s_ref[2 * p + 1])
        dq, dk, dv = attend_back(q_ref[p], k_ref[p], v_ref[p], do_ref[p], masks, None, sums)
        dq_ref[p] = dq
        dk_ref[p] = dk
        dv_ref[p] = dv

    for half, w, g in ((0, w_own, g_own), (1, w_oth, g_oth)):
        dq, dk, dv = three(dq_ref, half), three(dk_ref, half), three(dv_ref, half)
        g[1] = dot_tn(a_ref[...], dq).astype(BF16)
        g[2] = dot_tn(b_ref[...], dk).astype(BF16)
        g[3] = dot_tn(b_ref[...], dv).astype(BF16)
        part_a = dot_nt(dq, w[0])
        part_b = dot_nt(dk, w[1]) + dot_nt(dv, w[2])
        if half == 0:
            da_ref[...] = part_a
            db_ref[...] = part_b
        else:
            da_ref[...] += part_a
            db_ref[...] += part_b


def post_kernel(meta, x, gain, gain_cross, gm_ref, da_ref, db_ref, r_ref, n_ref, q_ref, k_ref, v_ref, t_ref, w_own, w_oth, o_own, o_oth, gt_ref, g_own, g_oth, gg_ref, bias, do_ref, dq_ref, dk_ref, dv_ref, gh_ref):
    @pl.when(meta[0] == 0)
    def _():
        back, gain_grad = norm_back(x[...].astype(F32), gain[0:1, :], da_ref[...] + db_ref[...])
        gt_ref[...] = gm_ref[...] + back
        gg_ref[0:1, :] = gain_grad
        gg_ref[1:2, :] = jnp.zeros_like(gain_grad)

    @pl.when(meta[0] == 1)
    def _():
        caption_bias(meta, bias)
        back, gain_grad = norm_back(r_ref[...], gain_cross[...], da_ref[...])
        gg_ref[1:2, :] = gain_grad
        gh_ref[...] = gm_ref[...] + back
        low = gh_ref[...].astype(BF16)
        for half, o, g in ((0, o_own, g_own), (1, o_oth, g_oth)):
            g[0] = dot_tn(low, three(t_ref, half)).astype(BF16)
            rows = dot_nt(low, o[...]).astype(BF16)
            for p in range(3):
                do_ref[3 * half + p] = rows[:, p * 128 : (p + 1) * 128]
        masks = head_masks()

        @pl.loop(0, 6)
        def _(p):
            for g in range(3):
                at = slice(g * GROUP, (g + 1) * GROUP)
                dq, dk, dv = attend_back(
                    q_ref[p, at], k_ref[p, at], v_ref[p, at], do_ref[p, at], masks, bias[g], None
                )
                dq_ref[p, at] = dq
                dk_ref[p, at] = dk
                dv_ref[p, at] = dv

        total = None
        for half, w, g in ((0, w_own, g_own), (1, w_oth, g_oth)):
            for j, ref in enumerate((dq_ref, dk_ref, dv_ref)):
                rows = three(ref, half)
                g[1 + j] = dot_tn(n_ref[...], rows).astype(BF16)
                part = dot_nt(rows, w[j])
                total = part if total is None else total + part
        back, gain_grad = norm_back(x[...].astype(F32), gain[0:1, :], total)
        gt_ref[...] = gh_ref[...] + back
        gg_ref[0:1, :] = gain_grad


def gather_kernel(table_sizes, out_sizes, idx, *refs):
    tables = refs[: len(table_sizes)]
    outs = refs[len(table_sizes) : len(table_sizes) + len(out_sizes)]
    sems = refs[-1]
    at = 0
    waits = []
    for out, size in zip(outs, out_sizes):
        for row in range(size):
            code = idx[at]
            base = 0
            for table, count in zip(tables, table_sizes):

                @pl.when((code >= base) & (code < base + count))
                def _():
                    pltpu.make_async_copy(table.at[code - base], out.at[row], sems.at[at]).start()

                base += count
            waits.append(pltpu.make_async_copy(tables[0].at[0], out.at[row], sems.at[at]))
            at += 1
    for wait in waits:
        wait.wait()


def gather_slots(idx, tables, out_sizes):
    sizes = tuple(table.shape[0] for table in tables)
    block = tables[0].shape[1:]
    return pl.pallas_call(
        functools.partial(gather_kernel, sizes, tuple(out_sizes)),
        out_shape=[jax.ShapeDtypeStruct((n,) + block, tables[0].dtype) for n in out_sizes],
        in_specs=[SMEM] + [ANY] * len(tables),
        out_specs=[ANY] * len(out_sizes),
        scratch_shapes=[pltpu.SemaphoreType.DMA((sum(out_sizes),))],
        name="gather_slots",
    )(idx, *tables)


def call(kernel, name, outs, scratch, smem_first, *args):
    return pl.pallas_call(
        kernel,
        out_shape=[jax.ShapeDtypeStruct(shape, dtype) for shape, dtype in outs],
        in_specs=([SMEM] if smem_first else []) + [VMEM] * (len(args) - int(smem_first)),
        out_specs=[VMEM] * len(outs),
        scratch_shapes=scratch,
        compiler_params=pltpu.CompilerParams(vmem_limit_bytes=LIMIT),
        name=name,
    )(*args)


def ffn_call(last, ffn_in, cot, up, down, *extra):
    rows, width = ffn_in.shape
    hidden = up.shape[1]
    chunk = hidden // 3
    whole = pl.BlockSpec((rows, width), lambda j: (0, 0))
    in_specs = [
        whole,
        whole,
        pl.BlockSpec((width, chunk), lambda j: (0, j)),
        pl.BlockSpec((chunk, width), lambda j: (j, 0)),
    ]
    g_spec = pl.BlockSpec((2, width, chunk), lambda j: (0, 0, j))
    g_shape = jax.ShapeDtypeStruct((2, width, hidden), BF16)
    wide = jax.ShapeDtypeStruct((rows, width), F32)
    if last:
        in_specs += [whole, whole, whole, pl.BlockSpec(extra[3].shape, lambda j: (0, 0))]
        out_shape = [g_shape, jax.ShapeDtypeStruct((rows, width), BF16), wide, jax.ShapeDtypeStruct((1, width), F32)]
        out_specs = [g_spec, whole, whole, pl.BlockSpec((1, width), lambda j: (0, 0))]
        scratch = [pltpu.VMEM((rows, width), F32)] * 2
    else:
        out_shape = [g_shape, wide, wide]
        out_specs = [g_spec, whole, whole]
        scratch = []
    return pl.pallas_call(
        functools.partial(ffn_kernel, last),
        grid=(3,),
        out_shape=out_shape,
        in_specs=in_specs,
        out_specs=out_specs,
        scratch_shapes=scratch,
        compiler_params=pltpu.CompilerParams(vmem_limit_bytes=LIMIT),
        name="ffn_own" if last else "ffn_other",
    )(ffn_in, cot, up, down, *extra)


def swap_mp(value, captions_only=False):
    if not captions_only:
        return lax.ppermute(value, "mp", [(0, 1), (1, 0)])
    count = lax.axis_size("dp")
    pairs = [((count + d) * 2 + c, (count + d) * 2 + 1 - c) for d in range(count) for c in range(2)]
    return lax.ppermute(value, ("half", "dp", "mp"), pairs)


def caption_shift(value, steps):
    count = lax.axis_size("dp")
    pairs = [
        ((count + d) * 2 + c, (count + (d + steps) % count) * 2 + c) for d in range(count) for c in range(2)
    ]
    return lax.ppermute(value, ("half", "dp", "mp"), pairs)


def reduce_dp(own, arrived):
    count = lax.axis_size("dp")
    me = lax.axis_index("dp")
    lead, rows, cols = own.shape
    bits = count.bit_length() - 1
    shape = (lead,) + (2,) * bits + (rows // count, cols)
    kept, got = own.reshape(shape), arrived.reshape(shape)
    for bit in range(bits):
        axis = bits - bit
        mine = (me >> bit) & 1

        def part(value, which):
            return lax.dynamic_index_in_dim(value, which, axis, keepdims=False).astype(F32)

        send = (part(kept, 1 - mine) + part(got, 1 - mine)).astype(BF16)
        kept = part(kept, mine) + part(got, mine)
        got = lax.ppermute(send, "dp", [(d, d ^ (1 << bit)) for d in range(count)])
        if bit < bits - 1:
            continue
    return kept + got.astype(F32)


def route_tables(slot_image, slot_length, me, c, side, cap_dev):
    total = slot_image.shape[0]
    count = total // cap_dev
    slot = jnp.arange(total)
    home = slot // cap_dev
    filled = slot_length > 0
    image = slot_image
    dest = image // IMG_DEV
    offset = jnp.where(filled, (home - dest) % count, SPREAD)
    core = image % IMG_DEV
    before = slot[None, :] < slot[:, None]
    same_home = home[None, :] == home[:, None]
    same_offset = offset[None, :] == offset[:, None]
    rank = jnp.sum((before & same_home & same_offset).astype(jnp.int32), axis=1)
    place = jnp.sum(
        (before & filled[None, :] & (image[None, :] == image[:, None])).astype(jnp.int32), axis=1
    )
    half_cap = QCAP // 2
    local = slot % cap_dev
    pack_core, pack_row = rank // half_cap, rank % half_cap
    seats = jnp.arange(half_cap)

    def pick(match, code):
        return jnp.sum(jnp.where(match, code[None, :], 0), axis=1)

    offs = jnp.repeat(jnp.arange(1, SPREAD), half_cap)
    rows = jnp.tile(seats, SPREAD - 1)
    mine = (offset[None, :] == offs[:, None]) & (pack_core[None, :] == c) & (pack_row[None, :] == rows[:, None])
    send_idx = pick(mine & (home[None, :] == me), local)
    per_core = cap_dev // 2
    arrived_code = cap_dev + jnp.where(pack_core == c, 0, 9) + (offset - 1) * half_cap + pack_row
    seat = jnp.arange(per_core)
    named = filled & (image == me * IMG_DEV + c)
    hit = jnp.where(
        (seat < CAPS)[:, None],
        named[None, :] & (place[None, :] == seat[:, None]),
        ((~filled) & (home == me) & (rank == c))[None, :],
    )
    work_idx = pick(hit, jnp.where(offset % SPREAD == 0, local, arrived_code))
    work_len = pick(hit, slot_length)
    work_idx = jnp.where(side == 0, c * per_core + seat, work_idx)
    at_core = jnp.where(core == c, 0, per_core) + place
    back_idx = pick(mine & (home[None, :] == (me + offs[:, None]) % count), at_core)
    here = lax.dynamic_slice_in_dim(
        jnp.where(
            filled,
            jnp.where(offset == 0, at_core, cap_dev + jnp.where(pack_core == c, 0, 9) + (offset - 1) * half_cap + pack_row),
            jnp.where(rank == c, 0, per_core) + per_core - 1,
        ),
        me * cap_dev,
        cap_dev,
    )
    spot = jnp.arange(cap_dev)
    home_idx = jnp.where(side == 0, jnp.where(spot // per_core == c, 0, per_core) + spot % per_core, here)
    return send_idx, work_idx, work_len, back_idx, home_idx


def shards(
    tokens,
    qkv_weight,
    out_weight,
    up_weight,
    down_weight,
    norm_gains,
    cross_gain,
    cross_query_matrix,
    cross_keyval,
    cross_out,
    slot_image,
    slot_length,
    cotangent,
):
    count = lax.axis_size("dp")
    side = lax.axis_index("half")
    me = lax.axis_index("dp")
    c = lax.axis_index("mp")
    row_count, width = tokens.shape[1:]
    cap_dev = row_count // SLOT
    per_core = cap_dev // 2
    rows = row_count // 2
    is_image = side == 0

    send_idx, work_idx, work_len, back_idx, home_idx = route_tables(
        slot_image, slot_length, me, c, side, cap_dev
    )
    meta = jnp.concatenate([side[None].astype(jnp.int32), work_len.astype(jnp.int32)])
    home_tokens = tokens[0].reshape(cap_dev, SLOT, width)
    home_cot = cotangent[0].reshape(cap_dev, SLOT, width)

    def travel(table):
        packs = gather_slots(send_idx, [table], [QCAP // 2] * (SPREAD - 1))
        got = [caption_shift(pack, -(o + 1)) for o, pack in enumerate(packs)]
        return got

    def settle(table, got):
        other = [swap_mp(g, True) for g in got]
        return gather_slots(work_idx, [table] + got + other, [per_core])[0].reshape(rows, width)

    got_tokens = travel(home_tokens)
    image_rows = lax.dynamic_slice_in_dim(tokens[0], c * rows, rows)
    pairs = [(2 * d + k, 2 * (count + d) + k) for d in range(count) for k in range(2)]
    image_here = lax.ppermute(image_rows, ("half", "dp", "mp"), pairs)
    got_cot = travel(home_cot)

    qkv = jnp.transpose(qkv_weight[0], (1, 0, 2))
    cross = jnp.stack([cross_query_matrix, cross_keyval[:, 0], cross_keyval[:, 1]])
    gen_own = jnp.where(is_image, qkv, cross)
    gen_out_own = jnp.where(is_image, out_weight[0], cross_out)
    gen_oth = swap_mp(gen_own)
    gen_out_oth = swap_mp(gen_out_own)
    qkv_oth = swap_mp(qkv, True)
    out_oth = swap_mp(out_weight[0], True)
    up_oth = swap_mp(up_weight[0])
    down_oth = swap_mp(down_weight[0])

    x = settle(home_tokens, got_tokens)
    cot = settle(home_cot, got_cot)
    gains = norm_gains[0]
    gain_cross = cross_gain[None]
    heads_shape = ((6, rows, 128), BF16)
    wide, narrow = ((rows, width), F32), ((rows, width), BF16)
    head_scratch = pltpu.VMEM((6, rows, 128), BF16)
    bias_scratch = pltpu.VMEM((3, GROUP, GROUP), F32)
    a, r, normed, sq, sk, sv, st = call(
        pre_kernel,
        "pre",
        [narrow, wide, narrow, heads_shape, heads_shape, heads_shape, heads_shape],
        [bias_scratch],
        True,
        meta, x, gains, gain_cross, qkv, qkv_oth, out_weight[0], out_oth,
    )
    b = jnp.where(is_image, a, image_here)
    q, k, v, ctx, sums, mixed, ffn_in = call(
        mid_kernel,
        "mid",
        [heads_shape, heads_shape, heads_shape, heads_shape, ((12, 1, rows), F32), wide, narrow],
        [],
        True,
        meta, a, b, r, gains, gen_own, gen_oth, gen_out_own, gen_out_oth,
    )
    ffn_g_oth, acc_out, acc_grad = ffn_call(False, ffn_in, cot, up_oth, down_oth)
    ffn_arrived = swap_mp(ffn_g_oth)
    ffn_g_own, y, gm, gain_ffn = ffn_call(True, ffn_in, cot, up_weight[0], down_weight[0], acc_out, acc_grad, mixed, gains)
    ffn_sum = reduce_dp(ffn_g_own, ffn_arrived)

    g_own, g_oth, da, db = call(
        back_kernel,
        "back",
        [((4, width, width // 2), BF16), ((4, width, width // 2), BF16), wide, wide],
        [head_scratch] * 4,
        True,
        meta, gm, ctx, sums, q, k, v, a, b, gen_own, gen_oth, gen_out_own, gen_out_oth,
    )
    gen_sum = reduce_dp(g_own, swap_mp(g_oth))
    image_part = lax.ppermute(db.astype(BF16), ("half", "dp", "mp"), [(d, s) for s, d in pairs])

    gt, g3_own, g3_oth, gain_two = call(
        post_kernel,
        "post",
        [wide, ((4, width, width // 2), BF16), ((4, width, width // 2), BF16), ((2, width), F32)],
        [bias_scratch] + [head_scratch] * 4 + [pltpu.VMEM((rows, width), F32)],
        True,
        meta, x, gains, gain_cross, gm, da, db, r, normed, sq, sk, sv, st, qkv, qkv_oth, out_weight[0], out_oth,
    )
    cap_sum = reduce_dp(g3_own, swap_mp(g3_oth))
    grad_rows = jnp.where(is_image, gt + image_part.astype(F32), gt).astype(BF16)

    def go_home(values):
        own = values.reshape(per_core, SLOT, width)
        other = swap_mp(own)
        packs = gather_slots(back_idx, [own, other], [QCAP // 2] * (SPREAD - 1))
        got = [caption_shift(pack, o + 1) for o, pack in enumerate(packs)]
        more = [swap_mp(g, True) for g in got]
        return gather_slots(home_idx, [own, other] + got + more, [cap_dev])[0].reshape(row_count, width)

    layer_out = go_home(y)
    grad_tokens = go_home(grad_rows).astype(F32)

    zero = jnp.zeros_like(gain_ffn)
    mine = jnp.concatenate([gain_two[0:1], gain_ffn])
    none = jnp.zeros_like(mine)
    gain_rows = jnp.concatenate(
        [jnp.where(is_image, mine, none), jnp.where(is_image, none, mine), gain_two[1:2]]
    )
    gain_rows = lax.psum(gain_rows, ("half", "dp", "mp"))
    part = width // count
    gain_rows = lax.dynamic_slice_in_dim(gain_rows, me * part, part, axis=1)
    sum_gains = jnp.where(is_image, gain_rows[0:2], gain_rows[2:4])
    sum_cross_gain = gain_rows[4]

    cross_low = gen_sum.astype(BF16)
    cross_arrived = lax.ppermute(cross_low, ("half", "dp", "mp"), [(d, s) for s, d in pairs])
    cross_sum = jnp.where(is_image, cross_arrived, cross_low).astype(F32)
    tower_sum = jnp.where(is_image, gen_sum, cap_sum)
    return (
        layer_out[None],
        grad_tokens[None],
        jnp.transpose(tower_sum[1:4], (1, 0, 2))[None],
        tower_sum[0].T[None],
        ffn_sum[0][None],
        ffn_sum[1].T[None],
        sum_gains[None],
        sum_cross_gain,
        cross_sum[1],
        jnp.stack([cross_sum[2], cross_sum[3]], axis=1),
        cross_sum[0].T,
    )


def solution(mesh):
    placed = (
        P("half", "dp", None),
        P("half", None, None, "mp"),
        P("half", "mp", None),
        P("half", None, "mp"),
        P("half", "mp", None),
        P("half", None, None),
        P(),
        P(None, "mp"),
        P(None, None, "mp"),
        P("mp", None),
        P(),
        P(),
        P("half", "dp", None),
    )
    return jax.shard_map(
        shards,
        mesh=mesh,
        in_specs=placed,
        out_specs=(
            P("half", "dp", None),
            P("half", "dp", None),
            P("half", "dp", None, "mp"),
            P("half", "mp", "dp"),
            P("half", "dp", "mp"),
            P("half", "mp", "dp"),
            P("half", None, "dp"),
            P("dp"),
            P("dp", "mp"),
            P("dp", None, "mp"),
            P("mp", "dp"),
        ),
        check_vma=False,
    )
```

time: 1450 us -> 786 us (0.54)
  waiting for transfers between devices: 666 us -> 146 us
  Pallas kernels: 0 us -> 415 us
  matrix products: 321 us -> 0 us
  local copies, waits for them, and re-layouts: 136 us -> 16.2 us
  other arithmetic: 145 us -> 38.1 us
  starting transfers between devices: 40.3 us -> 96.5 us
  blocking collectives: 106 us -> 62.5 us
  between operations: 17.5 us -> 2.08 us
    reduce_scatter x13 -> x0, waiting for transfers between devices: 488 us -> none  [the longest x1 99.7 us: shards(): lax.psum_scatter(grad_down, 'dp', scatter_dimension=1, tiled=True)]
    pallas_call x0 -> x14, Pallas kernels: none -> 415 us  [the longest x8 283 us: gather_slots(): pl.pallas_call(functools.partial(gather_kernel, sizes, tuple(out_sizes)),...]
    dot_general x67 -> x0, matrix products: 321 us -> none  [the longest x4 74.8 us: shards(): jnp.einsum('ci,cpkhe->ipkhe', matches, jnp.stack([grad_key, grad_value],...]
    unnamed x1 -> x0, blocking collectives: 101 us -> none
    ppermute x16 -> x47, starting transfers between devices: 38.4 us -> 96.5 us  [the longest x12 41.5 us: caption_shift(): return lax.ppermute(value, ('half', 'dp', 'mp'), pairs)]
    psum x1, blocking collectives: 4.93 us -> 62.5 us  [shards(): gain_rows = lax.psum(gain_rows, ('half', 'dp', 'mp'))]
    all_gather x7 -> x0, waiting for transfers between devices: 53.3 us -> none  [row_total(): return lax.all_gather(shares, 'mp', axis=0, tiled=True)]
    another operation x16 -> x1, other arithmetic: 44.3 us -> 0.02 us  [shards(): jnp.stack([cross_sum[2], cross_sum[3]], axis=1)]
  transfers between devices with their start and end apart: 37 -> 47, of which waited for: 23 -> 11; matrix products, arithmetic and copies ran while one was open for 28% -> 6% of each run, Pallas kernels for 0% -> 48%
where the time goes in v1:
time: 786 us; the launch traced here: 776 us
  Pallas kernels  415 us (53%)
  waiting for transfers between devices  146 us (19%)
  starting transfers between devices  96.5 us (12%)
  blocking collectives  62.5 us (8%)
  other arithmetic  38.1 us (5%)
  local copies, waits for them, and re-layouts  16.2 us (2%)
    pallas_call x8, Pallas kernels, gather_slots(): pl.pallas_call(functools.partial(gather_kernel, sizes, tuple(out_sizes)),...  283 us
    pallas_call x4, Pallas kernels, call(): pl.pallas_call(kernel, out_shape=[jax.ShapeDtypeStruct(shape, dtype) for...  101 us
    psum x1, blocking collectives, shards(): gain_rows = lax.psum(gain_rows, ('half', 'dp', 'mp'))  62.5 us
    ppermute x12, waiting for transfers between devices, caption_shift(): return lax.ppermute(value, ('half', 'dp', 'mp'), pairs)  61.8 us
    ppermute x9, waiting for transfers between devices, reduce_dp(): got = lax.ppermute(send, 'dp', [(d, d ^ 1 << bit) for d in range(count)])  59.3 us
    ppermute x12, starting transfers between devices, caption_shift(): return lax.ppermute(value, ('half', 'dp', 'mp'), pairs)  41.5 us
    pallas_call x2, Pallas kernels, ffn_call(): pl.pallas_call(functools.partial(ffn_kernel, last), grid=(3,), out_shape=...  30.7 us
    ppermute x14, starting transfers between devices, swap_mp(): return lax.ppermute(value, ('half', 'dp', 'mp'), pairs)  29.1 us
  transfers between devices with their start and end apart: 47, of which 11 were waited for; matrix products, arithmetic and copies ran while one was open for 6% of the time, Pallas kernels for 48%

profile of v1, /device:TPU:4, one launch (start us, length us, event | category | flops | bytes accessed | tf_op | source)
XLA Modules:
  0.0 776.3 jit_solution(13766775569831008828)
XLA Ops:
  6.6 28.8 %gather_slots.8 = (bf16[3,64,768]{2,1,0:T(8,128)(2,1)}, bf16[3,64,768]{2,1,0:T(8,128)(2,1)}, bf16[3,64,768]{2,1,0:T(8,128)(2,1)}) custom-call(s32[9]{0:T(128)} %get-tuple-element.116.idx, bf16[18,64,768]{2,1,0:T(8,128)(2,1)} %bitcast.155), custom_call_target="tpu_custom_call" | custom-call | tf_op jit(solution)/shard_map/gather_slots/pallas_call | solution.py:340
  35.4 6.4 collective-permute-start
  46.1 28.7 %gather_slots.10 = (bf16[3,64,768]{2,1,0:T(8,128)(2,1)}, bf16[3,64,768]{2,1,0:T(8,128)(2,1)}, bf16[3,64,768]{2,1,0:T(8,128)(2,1)}) custom-call(s32[9]{0:T(128)} %get-tuple-element.116.idx, bf16[18,64,768]{2,1,0:T(8,128)(2,1)} %bitcast.164), custom_call_target="tpu_custom_call" | custom-call | tf_op jit(solution)/shard_map/gather_slots/pallas_call | solution.py:340
  74.8 3.7 collective-permute-start.11
  78.5 5.5 collective-permute-start.12
  106.0 4.3 collective-permute-done.14.refs_4_
  124.7 28.6 %gather_slots.9 = bf16[9,64,768]{2,1,0:T(8,128)(2,1)} custom-call(s32[9]{0:T(128)} %broadcast_select_fusion.4.idx, bf16[18,64,768]{2,1,0:T(8,128)(2,1)} %bitcast.156, bf16[3,64,768]{2,1,0:T(8,128)(2,1)} %copy-done.12, bf16[3,64,768]{2,1,0:T(8,128)(2,1)} %copy-done.13, bf16[3,64,768]{2,1,0:T(8,128)(2,1)} %collective-permute-done.2.refs_3_, ...), custom_call_target="tpu_custom_call" | custom-call | tf_op jit(solution)/shard_map/gather_slots/pallas_call | solution.py:340
  153.3 28.7 %gather_slots.11 = bf16[9,64,768]{2,1,0:T(8,128)(2,1)} custom-call(s32[9]{0:T(128)} %broadcast_select_fusion.4.idx, bf16[18,64,768]{2,1,0:T(8,128)(2,1)} %bitcast.165, bf16[3,64,768]{2,1,0:T(8,128)(2,1)} %collective-permute-done.11.refs_1_, bf16[3,64,768]{2,1,0:T(8,128)(2,1)} %collective-permute-done.12.refs_2_, ...), custom_call_target="tpu_custom_call" | custom-call | tf_op jit(solution)/shard_map/gather_slots/pallas_call | solution.py:340
  182.0 20.4 %pre.1 = (bf16[576,768]{1,0:T(8,128)(2,1)}, f32[576,768]{1,0:T(8,128)}, bf16[576,768]{1,0:T(8,128)(2,1)}, bf16[6,576,128]{2,1,0:T(8,128)(2,1)}, bf16[6,576,128]{...) custom-call(s32[10]{0:T(128)} %pad_add_fusion.meta, bf16[576,768]{1,0:T(8,128)(2,1)} %bitcast.159, ...), custom_call_target="tpu_custom_call" | custom-call | tf_op jit(solution)/shard_map/pre/pallas_call | solution.py:351
  205.4 19.0 %mid.1 = (bf16[6,576,128]{2,1,0:T(8,128)(2,1)}, bf16[6,576,128]{2,1,0:T(8,128)(2,1)}, bf16[6,576,128]{2,1,0:T(8,128)(2,1)}, bf16[6,576,128]{2,1,0:T(8,128)(2,1)}...) custom-call(s32[10]{0:T(128)} %pad_add_fusion.meta, ...), custom_call_target="tpu_custom_call" | custom-call | tf_op jit(solution)/shard_map/mid/pallas_call | solution.py:351
  224.4 13.5 %ffn_other.1 = (bf16[2,768,1536]{2,1,0:T(8,128)(2,1)}, f32[576,768]{1,0:T(8,128)}, f32[576,768]{1,0:T(8,128)}) custom-call(bf16[576,768]{1,0:T(8,128)(2,1)} %get-tuple-element.57.f_ref, bf16[576,768]{1,0:T(8,128)(2,1)} %bitcast.157, bf16[768,1536]{1,0:T(8,128)(2,1)} %collective-permute-done.17.up, bf16[1536,768]{1,0:T(8,128)(2,1)} %collective-permute-done.18.down), custom_call_target="tpu_custom_call" | custom-call | tf_op jit(solution)/shard_map/ffn_other/pallas_call | solution.py:385
  238.2 17.2 %ffn_own.1 = (bf16[2,768,1536]{2,1,0:T(8,128)(2,1)}, bf16[576,768]{1,0:T(8,128)(2,1)}, f32[576,768]{1,0:T(8,128)}, f32[1,768]{1,0:T(1,128)}) custom-call(bf16[576,768]{1,0:T(8,128)(2,1)} %get-tuple-element.57.f_ref, bf16[576,768]{1,0:T(8,128)(2,1)} %bitcast.158, bf16[768,1536]{1,0:T(8,128)(2,1)} %bitcast.179, bf16[1536,768]{1,0:T(8,128)(2,1)} %bitcast.181, ...), custom_call_target="tpu_custom_call" | custom-call | tf_op jit(solution)/shard_map/ffn_own/pallas_call | solution.py:385
  255.3 28.6 %back.1 = (bf16[4,768,384]{2,1,0:T(8,128)(2,1)}, bf16[4,768,384]{2,1,0:T(8,128)(2,1)}, f32[576,768]{1,0:T(8,128)}, f32[576,768]{1,0:T(8,128)}) custom-call(s32[10]{0:T(128)} %pad_add_fusion.meta, f32[576,768]{1,0:T(8,128)} %get-tuple-element.68.gm_ref, bf16[6,576,128]{2,1,0:T(8,128)(2,1)} %get-tuple-element.69.c_ref, f32[12,1,576]{2,1,0:T(1,128)} %get-tuple-element.70.s_ref, ...), custom_call_target="tpu_custom_call" | custom-call | tf_op jit(solution)/shard_map/back/pallas_call | solution.py:351
  283.9 33.1 %post.1 = (f32[576,768]{1,0:T(8,128)}, bf16[4,768,384]{2,1,0:T(8,128)(2,1)}, bf16[4,768,384]{2,1,0:T(8,128)(2,1)}, f32[2,768]{1,0:T(2,128)}) custom-call(s32[10]{0:T(128)} %pad_add_fusion.meta, bf16[576,768]{1,0:T(8,128)(2,1)} %bitcast.160, f32[2,768]{1,0:T(2,128)} %bitcast.187, f32[1,768]{1,0:T(1,128)} %broadcast_in_dim.126.gain_cross, ...), custom_call_target="tpu_custom_call" | custom-call | tf_op jit(solution)/shard_map/post/pallas_call | solution.py:351
  319.9 18.9 %collective-permute-done.26 = bf16[576,768]{1,0:T(8,128)(2,1)S(1)} collective-permute-done((bf16[576,768]{1,0:T(8,128)(2,1)S(1)}, bf16[576,768]{1,0:T(8,128)(2,1)S(1)}, u32[]{:S(2)}, u32[]{:S(2)}) %collective-permute-start.26) | collective-permute-done | bytes 884768 | tf_op jit(solution)/shard_map/ppermute | solution.py:589
  343.1 9.2 %collective-permute-start.39 = (bf16[4,2,2,96,384]{4,3,0,1,2:T(8,128)(2,1)}, bf16[4,2,2,96,384]{4,3,0,1,2:T(8,128)(2,1)}, u32[]{:S(2)}, u32[]{:S(2)}) collective-permute-start(bf16[4,2,2,96,384]{4,3,0,1,2:T(8,128)(2,1)} %fusion.4), channel_id=1, source_target_pairs={{0,2},{2,0},{4,6},{6,4},{8,10},{10,8},{12,14},{14,12},{1,3},{3,1},... | collective-permute-start | bytes 3538952 | tf_op jit(solution)/shard_map/ppermute | solution.py:429
  352.3 62.5 %psum.7 = f32[5,768]{1,0:T(8,128)} all-reduce(f32[5,768]{1,0:T(8,128)S(1)} %pad_maximum_fusion.1), channel_id=1, replica_groups=mesh['half'=2,'dp'=8,'mp'=2] {'half','dp','mp'}, use_global_device_ids=true, to_apply=%region_6.7 | all-reduce | flops 3840 | bytes 30720 | tf_op jit(solution)/shard_map/psum | solution.py:619
  414.8 28.6 %gather_slots.12 = (bf16[3,64,768]{2,1,0:T(8,128)(2,1)}, bf16[3,64,768]{2,1,0:T(8,128)(2,1)}, bf16[3,64,768]{2,1,0:T(8,128)(2,1)}) custom-call(s32[9]{0:T(128)} %get-tuple-element.115.idx, bf16[9,64,768]{2,1,0:T(8,128)(2,1)} %bitcast.171, bf16[9,64,768]{2,1,0:T(8,128)(2,1)} %collective-permute-done.19.refs_1_), custom_call_target="tpu_custom_call" | custom-call | tf_op jit(solution)/shard_map/gather_slots/pallas_call | solution.py:340
  445.6 3.5 collective-permute-start.21
  449.2 28.7 %gather_slots.14 = (bf16[3,64,768]{2,1,0:T(8,128)(2,1)}, bf16[3,64,768]{2,1,0:T(8,128)(2,1)}, bf16[3,64,768]{2,1,0:T(8,128)(2,1)}) custom-call(s32[9]{0:T(128)} %get-tuple-element.115.idx, bf16[9,64,768]{2,1,0:T(8,128)(2,1)} %bitcast.162, bf16[9,64,768]{2,1,0:T(8,128)(2,1)} %copy-done.7), custom_call_target="tpu_custom_call" | custom-call | tf_op jit(solution)/shard_map/gather_slots/pallas_call | solution.py:340
  484.9 3.8 collective-permute-start.22
  490.6 3.8 fusion
  497.2 4.9 collective-permute-done.22.refs_4_
  512.9 6.3 collective-permute-start.30
  519.2 55.6 %collective-permute-done.28.refs_2_ = bf16[3,64,768]{2,1,0:T(8,128)(2,1)S(1)} collective-permute-done((bf16[3,64,768]{2,1,0:T(8,128)(2,1)S(1)}, bf16[3,64,768]{2,1,0:T(8,128)(2,1)S(1)}, u32[]{:S(2)}, u32[]{:S(2)}) %collective-permute-start.28) | collective-permute-done | bytes 294944 | tf_op jit(solution)/shard_map/ppermute | solution.py:410
  586.9 55.5 %gather_slots.13 = bf16[18,64,768]{2,1,0:T(8,128)(2,1)} custom-call(s32[18]{0:T(128)} %broadcast_select_fusion.5.idx, bf16[9,64,768]{2,1,0:T(8,128)(2,1)} %bitcast.172, bf16[9,64,768]{2,1,0:T(8,128)(2,1)} %collective-permute-done.19.refs_1_, bf16[3,64,768]{2,1,0:T(8,128)(2,1)} %copy-done.14, bf16[3,64,768]{2,1,0:T(8,128)(2,1)} %copy-done.15, ...), custom_call_target="tpu_custom_call" | custom-call | tf_op jit(solution)/shard_map/gather_slots/pallas_call | solution.py:340
  642.4 55.5 %gather_slots.15 = bf16[18,64,768]{2,1,0:T(8,128)(2,1)} custom-call(s32[18]{0:T(128)} %broadcast_select_fusion.5.idx, bf16[9,64,768]{2,1,0:T(8,128)(2,1)} %bitcast.163, bf16[9,64,768]{2,1,0:T(8,128)(2,1)} %copy-done.7, bf16[3,64,768]{2,1,0:T(8,128)(2,1)} %copy-done.19, bf16[3,64,768]{2,1,0:T(8,128)(2,1)} %collective-permute-done.29.refs_3_, ...), custom_call_target="tpu_custom_call" | custom-call | tf_op jit(solution)/shard_map/gather_slots/pallas_call | solution.py:340
  701.2 3.1 convert_add_fusion
  709.9 10.8 %collective-permute-done.41 = bf16[4,96,384]{2,1,0:T(8,128)(2,1)S(1)} collective-permute-done((bf16[4,96,384]{2,1,0:T(8,128)(2,1)S(1)}, bf16[4,96,384]{2,1,0:T(8,128)(2,1)S(1)}, u32[]{:S(2)}, u32[]{:S(2)}) %collective-permute-start.41) | collective-permute-done | bytes 294944 | tf_op jit(solution)/shard_map/ppermute | solution.py:429
  720.6 6.2 collective-permute-done.37
  729.9 17.4 %collective-permute-done.44 = bf16[2,2,96,1536]{3,2,0,1:T(8,128)(2,1)S(1)} collective-permute-done((bf16[2,2,96,1536]{3,2,0,1:T(8,128)(2,1)S(1)}, bf16[2,2,96,1536]{3,2,0,1:T(8,128)(2,1)S(1)}, u32[]{:S(2)}, u32[]{:S(2)}) %collective-permute-start.44) | collective-permute-done | bytes 1179680 | tf_op jit(solution)/shard_map/ppermute | solution.py:429
  749.8 24.8 %collective-permute-done.45 = bf16[2,96,1536]{2,1,0:T(8,128)(2,1)S(1)} collective-permute-done((bf16[2,96,1536]{2,1,0:T(8,128)(2,1)S(1)}, bf16[2,96,1536]{2,1,0:T(8,128)(2,1)S(1)}, u32[]{:S(2)}, u32[]{:S(2)}) %collective-permute-start.45) | collective-permute-done | bytes 589856 | tf_op jit(solution)/shard_map/ppermute | solution.py:429
  (205 shorter events, 108.5 us)
Async XLA Ops:
  35.4 48.6 %collective-permute-start = (bf16[3,64,768]{2,1,0:T(8,128)(2,1)}, bf16[3,64,768]{2,1,0:T(8,128)(2,1)S(1)}, u32[]{:S(2)}, u32[]{:S(2)}) collective-permute-start(bf16[3,64,768]{2,1,0:T(8,128)(2,1)} %get-tuple-element.52), channel_id=1, source_target_pairs={{16,30},{17,31},{18,16},{19,17},{20,18},{21,19},{22,20},{23,21},{2... | collective-permute-start | bytes 884744 | tf_op jit(solution)/shard_map/ppermute | solution.py:410
  41.8 44.1 %collective-permute-start.1 = (bf16[3,64,768]{2,1,0:T(8,128)(2,1)}, bf16[3,64,768]{2,1,0:T(8,128)(2,1)S(1)}, u32[]{:S(2)}, u32[]{:S(2)}) collective-permute-start(bf16[3,64,768]{2,1,0:T(8,128)(2,1)} %get-tuple-element.53), channel_id=1, source_target_pairs={{16,28},{17,29},{18,30},{19,31},{20,16},{21,17},{22,18},{23,19},{2... | collective-permute-start | bytes 884744 | tf_op jit(solution)/shard_map/ppermute | solution.py:410
  44.2 43.7 %collective-permute-start.2 = (bf16[3,64,768]{2,1,0:T(8,128)(2,1)}, bf16[3,64,768]{2,1,0:T(8,128)(2,1)}, u32[]{:S(2)}, u32[]{:S(2)}) collective-permute-start(bf16[3,64,768]{2,1,0:T(8,128)(2,1)} %get-tuple-element.54), channel_id=1, source_target_pairs={{16,26},{17,27},{18,28},{19,29},{20,30},{21,31},{22,16},{23,17},{2... | collective-permute-start | bytes 884744 | tf_op jit(solution)/shard_map/ppermute | solution.py:410
  84.0 39.2 %collective-permute-start.6 = (bf16[3,768,384]{2,1,0:T(8,128)(2,1)S(1)}, bf16[3,768,384]{2,1,0:T(8,128)(2,1)}, u32[]{:S(2)}, u32[]{:S(2)}) collective-permute-start(bf16[3,768,384]{2,1,0:T(8,128)(2,1)S(1)} %bitcast.154), channel_id=1, source_target_pairs={{16,17},{17,16},{18,19},{19,18},{20,21},{21,20},{22,23},{23,22},{2... | collective-permute-start | bytes 5308424 | tf_op jit(solution)/shard_map/ppermute | solution.py:402
  100.6 123.8 %collective-permute-start.17 = (bf16[768,1536]{1,0:T(8,128)(2,1)}, bf16[768,1536]{1,0:T(8,128)(2,1)}, u32[]{:S(2)}, u32[]{:S(2)}) collective-permute-start(bf16[768,1536]{1,0:T(8,128)(2,1)} %bitcast.178), channel_id=1, source_target_pairs={{0,1},{1,0},{2,3},{3,2},{4,5},{5,4},{6,7},{7,6},{8,9},{9,8},{10,11... | collective-permute-start | bytes 7077896 | tf_op jit(solution)/shard_map/ppermute | solution.py:399
  101.0 123.4 %collective-permute-start.18 = (bf16[1536,768]{1,0:T(8,128)(2,1)}, bf16[1536,768]{1,0:T(8,128)(2,1)}, u32[]{:S(2)}, u32[]{:S(2)}) collective-permute-start(bf16[1536,768]{1,0:T(8,128)(2,1)} %bitcast.180), channel_id=1, source_target_pairs={{0,1},{1,0},{2,3},{3,2},{4,5},{5,4},{6,7},{7,6},{8,9},{9,8},{10,11... | collective-permute-start | bytes 7077896 | tf_op jit(solution)/shard_map/ppermute | solution.py:399
  105.8 98.8 %collective-permute-start.9 = (bf16[3,768,384]{2,1,0:T(8,128)(2,1)S(1)}, bf16[3,768,384]{2,1,0:T(8,128)(2,1)}, u32[]{:S(2)}, u32[]{:S(2)}) collective-permute-start(bf16[3,768,384]{2,1,0:T(8,128)(2,1)S(1)} %maximum_select_fusion.w_own), channel_id=1, source_target_pairs={{0,1},{1,0},{2,3},{3,2},{4,5},{5,4},{6,7},{7,6},{8,9},{9,8},{10,11... | collective-permute-start | bytes 5308424 | tf_op jit(solution)/shard_map/ppermute | solution.py:399
  118.4 84.0 %collective-permute-start.8 = (bf16[576,768]{1,0:T(8,128)(2,1)}, bf16[576,768]{1,0:T(8,128)(2,1)}, u32[]{:S(2)}, u32[]{:S(2)}) collective-permute-start(bf16[576,768]{1,0:T(8,128)(2,1)} %dynamic-slice_bitcast_fusion), channel_id=1, source_target_pairs={{0,16},{1,17},{2,18},{3,19},{4,20},{5,21},{6,22},{7,23},{8,24},{9,... | collective-permute-start | bytes 2654216 | tf_op jit(solution)/shard_map/ppermute | solution.py:536
  123.3 81.3 %collective-permute-start.10 = (bf16[384,768]{1,0:T(8,128)(2,1)}, bf16[384,768]{1,0:T(8,128)(2,1)S(1)}, u32[]{:S(2)}, u32[]{:S(2)}) collective-permute-start(bf16[384,768]{1,0:T(8,128)(2,1)} %broadcast_select_fusion.1.o_own), channel_id=1, source_target_pairs={{0,1},{1,0},{2,3},{3,2},{4,5},{5,4},{6,7},{7,6},{8,9},{9,8},{10,11... | collective-permute-start | bytes 1769480 | tf_op jit(solution)/shard_map/ppermute | solution.py:399
  237.9 250.7 %collective-permute-start.42 = (bf16[2,768,1536]{2,1,0:T(8,128)(2,1)}, bf16[2,768,1536]{2,1,0:T(8,128)(2,1)}, u32[]{:S(2)}, u32[]{:S(2)}) collective-permute-start(bf16[2,768,1536]{2,1,0:T(8,128)(2,1)} %get-tuple-element.90), channel_id=1, source_target_pairs={{0,1},{1,0},{2,3},{3,2},{4,5},{5,4},{6,7},{7,6},{8,9},{9,8},{10,11... | collective-permute-start | bytes 14155784 | tf_op jit(solution)/shard_map/ppermute | solution.py:399
  317.1 23.0 %collective-permute-start.38 = (bf16[4,768,384]{2,1,0:T(8,128)(2,1)}, bf16[4,768,384]{2,1,0:T(8,128)(2,1)}, u32[]{:S(2)}, u32[]{:S(2)}) collective-permute-start(bf16[4,768,384]{2,1,0:T(8,128)(2,1)} %get-tuple-element.88), channel_id=1, source_target_pairs={{0,1},{1,0},{2,3},{3,2},{4,5},{5,4},{6,7},{7,6},{8,9},{9,8},{10,11... | collective-permute-start | bytes 7077896 | tf_op jit(solution)/shard_map/ppermute | solution.py:399
  317.4 160.4 %collective-permute-start.34 = (bf16[4,768,384]{2,1,0:T(8,128)(2,1)}, bf16[4,768,384]{2,1,0:T(8,128)(2,1)}, u32[]{:S(2)}, u32[]{:S(2)}) collective-permute-start(bf16[4,768,384]{2,1,0:T(8,128)(2,1)} %get-tuple-element.86), channel_id=1, source_target_pairs={{0,1},{1,0},{2,3},{3,2},{4,5},{5,4},{6,7},{7,6},{8,9},{9,8},{10,11... | collective-permute-start | bytes 7077896 | tf_op jit(solution)/shard_map/ppermute | solution.py:399
  317.7 21.1 %collective-permute-start.26 = (bf16[576,768]{1,0:T(8,128)(2,1)S(1)}, bf16[576,768]{1,0:T(8,128)(2,1)S(1)}, u32[]{:S(2)}, u32[]{:S(2)}) collective-permute-start(bf16[576,768]{1,0:T(8,128)(2,1)S(1)} %convert_element_type.195), channel_id=1, source_target_pairs={{16,0},{17,1},{18,2},{19,3},{20,4},{21,5},{22,6},{23,7},{24,8},{25... | collective-permute-start | bytes 2654216 | tf_op jit(solution)/shard_map/ppermute | solution.py:589
  319.5 95.3 %collective-permute-start.19 = (bf16[9,64,768]{2,1,0:T(8,128)(2,1)S(1)}, bf16[9,64,768]{2,1,0:T(8,128)(2,1)}, u32[]{:S(2)}, u32[]{:S(2)}) collective-permute-start(bf16[9,64,768]{2,1,0:T(8,128)(2,1)S(1)} %bitcast.173), channel_id=1, source_target_pairs={{0,1},{1,0},{2,3},{3,2},{4,5},{5,4},{6,7},{7,6},{8,9},{9,8},{10,11... | collective-permute-start | bytes 2654216 | tf_op jit(solution)/shard_map/ppermute | solution.py:399
  339.0 106.5 %collective-permute-start.27 = (bf16[9,64,768]{2,1,0:T(8,128)(2,1)S(1)}, bf16[9,64,768]{2,1,0:T(8,128)(2,1)S(1)}, u32[]{:S(2)}, u32[]{:S(2)}) collective-permute-start(bf16[9,64,768]{2,1,0:T(8,128)(2,1)S(1)} %bitcast.161), channel_id=1, source_target_pairs={{0,1},{1,0},{2,3},{3,2},{4,5},{5,4},{6,7},{7,6},{8,9},{9,8},{10,11... | collective-permute-start | bytes 2654216 | tf_op jit(solution)/shard_map/ppermute | solution.py:399
  343.1 163.4 %collective-permute-start.39 = (bf16[4,2,2,96,384]{4,3,0,1,2:T(8,128)(2,1)}, bf16[4,2,2,96,384]{4,3,0,1,2:T(8,128)(2,1)}, u32[]{:S(2)}, u32[]{:S(2)}) collective-permute-start(bf16[4,2,2,96,384]{4,3,0,1,2:T(8,128)(2,1)} %fusion.4), channel_id=1, source_target_pairs={{0,2},{2,0},{4,6},{6,4},{8,10},{10,8},{12,14},{14,12},{1,3},{3,1},... | collective-permute-start | bytes 3538952 | tf_op jit(solution)/shard_map/ppermute | solution.py:429
  443.5 41.4 %collective-permute-start.20 = (bf16[3,64,768]{2,1,0:T(8,128)(2,1)}, bf16[3,64,768]{2,1,0:T(8,128)(2,1)S(1)}, u32[]{:S(2)}, u32[]{:S(2)}) collective-permute-start(bf16[3,64,768]{2,1,0:T(8,128)(2,1)} %get-tuple-element.65), channel_id=1, source_target_pairs={{16,18},{17,19},{18,20},{19,21},{20,22},{21,23},{22,24},{23,25},{2... | collective-permute-start | bytes 884744 | tf_op jit(solution)/shard_map/ppermute | solution.py:410
  445.6 48.8 %collective-permute-start.21 = (bf16[3,64,768]{2,1,0:T(8,128)(2,1)}, bf16[3,64,768]{2,1,0:T(8,128)(2,1)S(1)}, u32[]{:S(2)}, u32[]{:S(2)}) collective-permute-start(bf16[3,64,768]{2,1,0:T(8,128)(2,1)} %get-tuple-element.66), channel_id=1, source_target_pairs={{16,20},{17,21},{18,22},{19,23},{20,24},{21,25},{22,26},{23,27},{2... | collective-permute-start | bytes 884744 | tf_op jit(solution)/shard_map/ppermute | solution.py:410
  480.0 96.7 %collective-permute-start.35 = (bf16[4,2,2,96,384]{4,3,0,1,2:T(8,128)(2,1)S(1)}, bf16[4,2,2,96,384]{4,3,0,1,2:T(8,128)(2,1)S(1)}, u32[]{:S(2)}, u32[]{:S(2)}) collective-permute-start(bf16[4,2,2,96,384]{4,3,0,1,2:T(8,128)(2,1)S(1)} %fusion.3), channel_id=1, source_target_pairs={{0,2},{2,0},{4,6},{6,4},{8,10},{10,8},{12,14},{14,12},{1,3},{3,1},... | collective-permute-start | bytes 3538952 | tf_op jit(solution)/shard_map/ppermute | solution.py:429
  494.4 210.3 %collective-permute-start.43 = (bf16[2,2,2,96,1536]{4,3,0,1,2:T(8,128)(2,1)}, bf16[2,2,2,96,1536]{4,3,0,1,2:T(8,128)(2,1)}, u32[]{:S(2)}, u32[]{:S(2)}) collective-permute-start(bf16[2,2,2,96,1536]{4,3,0,1,2:T(8,128)(2,1)} %fusion), channel_id=1, source_target_pairs={{0,2},{2,0},{4,6},{6,4},{8,10},{10,8},{12,14},{14,12},{1,3},{3,1},... | collective-permute-start | bytes 7077896 | tf_op jit(solution)/shard_map/ppermute | solution.py:429
  506.5 68.3 %collective-permute-start.28 = (bf16[3,64,768]{2,1,0:T(8,128)(2,1)S(1)}, bf16[3,64,768]{2,1,0:T(8,128)(2,1)S(1)}, u32[]{:S(2)}, u32[]{:S(2)}) collective-permute-start(bf16[3,64,768]{2,1,0:T(8,128)(2,1)S(1)} %copy-done.29), channel_id=1, source_target_pairs={{16,18},{17,19},{18,20},{19,21},{20,22},{21,23},{22,24},{23,25},{2... | collective-permute-start | bytes 884744 | tf_op jit(solution)/shard_map/ppermute | solution.py:410
  510.8 67.4 %collective-permute-start.29 = (bf16[3,64,768]{2,1,0:T(8,128)(2,1)S(1)}, bf16[3,64,768]{2,1,0:T(8,128)(2,1)}, u32[]{:S(2)}, u32[]{:S(2)}) collective-permute-start(bf16[3,64,768]{2,1,0:T(8,128)(2,1)S(1)} %copy-done.28), channel_id=1, source_target_pairs={{16,20},{17,21},{18,22},{19,23},{20,24},{21,25},{22,26},{23,27},{2... | collective-permute-start | bytes 884744 | tf_op jit(solution)/shard_map/ppermute | solution.py:410
  512.9 67.9 %collective-permute-start.30 = (bf16[3,64,768]{2,1,0:T(8,128)(2,1)S(1)}, bf16[3,64,768]{2,1,0:T(8,128)(2,1)}, u32[]{:S(2)}, u32[]{:S(2)}) collective-permute-start(bf16[3,64,768]{2,1,0:T(8,128)(2,1)S(1)} %copy-done.27), channel_id=1, source_target_pairs={{16,22},{17,23},{18,24},{19,25},{20,26},{21,27},{22,28},{23,29},{2... | collective-permute-start | bytes 884744 | tf_op jit(solution)/shard_map/ppermute | solution.py:410
  576.7 121.3 %collective-permute-start.40 = (bf16[4,2,96,384]{3,2,0,1:T(8,128)(2,1)}, bf16[4,2,96,384]{3,2,0,1:T(8,128)(2,1)S(1)}, u32[]{:S(2)}, u32[]{:S(2)}) collective-permute-start(bf16[4,2,96,384]{3,2,0,1:T(8,128)(2,1)} %get-tuple-element.139), channel_id=1, source_target_pairs={{0,4},{2,6},{4,0},{6,2},{8,12},{10,14},{12,8},{14,10},{1,5},{3,7},... | collective-permute-start | bytes 1769480 | tf_op jit(solution)/shard_map/ppermute | solution.py:429
  578.2 121.3 %collective-permute-start.36 = (bf16[4,2,96,384]{3,2,0,1:T(8,128)(2,1)}, bf16[4,2,96,384]{3,2,0,1:T(8,128)(2,1)S(1)}, u32[]{:S(2)}, u32[]{:S(2)}) collective-permute-start(bf16[4,2,96,384]{3,2,0,1:T(8,128)(2,1)} %get-tuple-element.137), channel_id=1, source_target_pairs={{0,4},{2,6},{4,0},{6,2},{8,12},{10,14},{12,8},{14,10},{1,5},{3,7},... | collective-permute-start | bytes 1769480 | tf_op jit(solution)/shard_map/ppermute | solution.py:429
  580.7 61.7 %collective-permute-start.32 = (bf16[3,64,768]{2,1,0:T(8,128)(2,1)}, bf16[3,64,768]{2,1,0:T(8,128)(2,1)}, u32[]{:S(2)}, u32[]{:S(2)}) collective-permute-start(bf16[3,64,768]{2,1,0:T(8,128)(2,1)} %collective-permute-done.29.refs_3_), channel_id=1, source_target_pairs={{16,17},{17,16},{18,19},{19,18},{20,21},{21,20},{22,23},{23,22},{2... | collective-permute-start | bytes 884744 | tf_op jit(solution)/shard_map/ppermute | solution.py:402
  583.4 59.0 %collective-permute-start.33 = (bf16[3,64,768]{2,1,0:T(8,128)(2,1)}, bf16[3,64,768]{2,1,0:T(8,128)(2,1)}, u32[]{:S(2)}, u32[]{:S(2)}) collective-permute-start(bf16[3,64,768]{2,1,0:T(8,128)(2,1)} %collective-permute-done.30.refs_4_), channel_id=1, source_target_pairs={{16,17},{17,16},{18,19},{19,18},{20,21},{21,20},{22,23},{23,22},{2... | collective-permute-start | bytes 884744 | tf_op jit(solution)/shard_map/ppermute | solution.py:402
  698.1 22.5 %collective-permute-start.41 = (bf16[4,96,384]{2,1,0:T(8,128)(2,1)S(1)}, bf16[4,96,384]{2,1,0:T(8,128)(2,1)S(1)}, u32[]{:S(2)}, u32[]{:S(2)}) collective-permute-start(bf16[4,96,384]{2,1,0:T(8,128)(2,1)S(1)} %fusion.16), channel_id=1, source_target_pairs={{0,8},{2,10},{4,12},{6,14},{8,0},{10,2},{12,4},{14,6},{1,9},{3,11}... | collective-permute-start | bytes 884744 | tf_op jit(solution)/shard_map/ppermute | solution.py:429
  699.6 27.3 %collective-permute-start.37 = (bf16[4,96,384]{2,1,0:T(8,128)(2,1)S(1)}, bf16[4,96,384]{2,1,0:T(8,128)(2,1)S(1)}, u32[]{:S(2)}, u32[]{:S(2)}) collective-permute-start(bf16[4,96,384]{2,1,0:T(8,128)(2,1)S(1)} %fusion.15), channel_id=1, source_target_pairs={{0,8},{2,10},{4,12},{6,14},{8,0},{10,2},{12,4},{14,6},{1,9},{3,11}... | collective-permute-start | bytes 884744 | tf_op jit(solution)/shard_map/ppermute | solution.py:429
  707.3 39.9 %collective-permute-start.44 = (bf16[2,2,96,1536]{3,2,0,1:T(8,128)(2,1)S(1)}, bf16[2,2,96,1536]{3,2,0,1:T(8,128)(2,1)S(1)}, u32[]{:S(2)}, u32[]{:S(2)}) collective-permute-start(bf16[2,2,96,1536]{3,2,0,1:T(8,128)(2,1)S(1)} %get-tuple-element.127), channel_id=1, source_target_pairs={{0,4},{2,6},{4,0},{6,2},{8,12},{10,14},{12,8},{14,10},{1,5},{3,7},... | collective-permute-start | bytes 3538952 | tf_op jit(solution)/shard_map/ppermute | solution.py:429
  727.1 20.9 %collective-permute-start.46 = (bf16[4,96,384]{2,1,0:T(8,128)(2,1)S(1)}, bf16[4,96,384]{2,1,0:T(8,128)(2,1)S(1)}, u32[]{:S(2)}, u32[]{:S(2)}) collective-permute-start(bf16[4,96,384]{2,1,0:T(8,128)(2,1)S(1)} %get-tuple-element.133), channel_id=1, source_target_pairs={{16,0},{17,1},{18,2},{19,3},{20,4},{21,5},{22,6},{23,7},{24,8},{25... | collective-permute-start | bytes 884744 | tf_op jit(solution)/shard_map/ppermute | solution.py:626
  747.4 27.2 %collective-permute-start.45 = (bf16[2,96,1536]{2,1,0:T(8,128)(2,1)S(1)}, bf16[2,96,1536]{2,1,0:T(8,128)(2,1)S(1)}, u32[]{:S(2)}, u32[]{:S(2)}) collective-permute-start(bf16[2,96,1536]{2,1,0:T(8,128)(2,1)S(1)} %fusion.11), channel_id=1, source_target_pairs={{0,8},{2,10},{4,12},{6,14},{8,0},{10,2},{12,4},{14,6},{1,9},{3,11}... | collective-permute-start | bytes 1769480 | tf_op jit(solution)/shard_map/ppermute | solution.py:429
  (48 other events, 685.0 us)

commit v2 on v1

--- a/solution.py
+++ b/solution.py
@@ -394,6 +394,424 @@
     )(ffn_in, cot, up, down, *extra)
 
 
+MESH = pl.DeviceIdType.MESH
+STEPS = SPREAD - 1
+PACK = QCAP // 2
+
+
+class Links:
+    def __init__(self, send_sems, recv_sems):
+        self.send, self.recv, self.used = send_sems, recv_sems, 0
+
+    def copy(self, src, dst, device):
+        at = self.used
+        self.used += 1
+        return pltpu.make_async_remote_copy(
+            src_ref=src,
+            dst_ref=dst,
+            send_sem=self.send.at[at],
+            recv_sem=self.recv.at[at],
+            device_id=device,
+            device_id_type=MESH,
+        )
+
+
+def place(count):
+    side, me, c = lax.axis_index("half"), lax.axis_index("dp"), lax.axis_index("mp")
+    return side, me, c, lambda k: (side, lax.rem(me + k + count, count), c)
+
+
+def greet(both, captions, side):
+    barrier = pltpu.get_barrier_semaphore()
+    for device in both:
+        pl.semaphore_signal(barrier, inc=1, device_id=device, device_id_type=MESH)
+
+    @pl.when(side == 0)
+    def _():
+        pl.semaphore_wait(barrier, len(both))
+
+    @pl.when(side == 1)
+    def _():
+        for device in captions:
+            pl.semaphore_signal(barrier, inc=1, device_id=device, device_id_type=MESH)
+        pl.semaphore_wait(barrier, len(both) + len(captions))
+
+
+def choose(code, near, far):
+    split = near.shape[0]
+    a = near[jnp.minimum(code, split - 1)]
+    b = far[jnp.maximum(code - split, 0)]
+    return jnp.where(code < split, a, b)
+
+
+def route_kernel(count, send_idx, work_idx, home_t, home_c, qkv, out_w, gen, gen_out, up, down, x, cot, image, qkv_o, out_o, gen_o, gen_out_o, up_o, down_o, near_t, near_c, far_t, far_c, pack_t, pack_c, send_sems, recv_sems, local_sems):
+    side, me, c, along = place(count)
+    twin = (side, me, 1 - c)
+    across = (1 - side, me, c)
+    links = Links(send_sems, recv_sems)
+    slots = home_t.shape[0]
+    half = slots // 2
+    loads = [
+        pltpu.make_async_copy(home_t, near_t, local_sems.at[0]),
+        pltpu.make_async_copy(home_c, near_c, local_sems.at[1]),
+    ]
+    for load in loads:
+        load.start()
+    greet([twin, across], [along(k) for k in (-3, -2, -1, 1, 2, 3)], side)
+
+    first = [links.copy(gen, gen_o, twin), links.copy(gen_out, gen_out_o, twin)]
+    for copy in first:
+        copy.start()
+    picture = links.copy(home_t.at[pl.ds(c * half, half)], image, across)
+    late = [links.copy(up, up_o, twin), links.copy(down, down_o, twin)]
+    own = [links.copy(qkv, qkv_o, twin), links.copy(out_w, out_o, twin)]
+    hops = []
+    for far, pack in ((far_t, pack_t), (far_c, pack_c)):
+        for o in range(STEPS):
+            there = far.at[pl.ds(PACK * o, PACK)]
+            hops.append(
+                (
+                    links.copy(pack.at[o], there, along(-o - 1)),
+                    links.copy(there, far.at[pl.ds(PACK * (STEPS + o), PACK)], twin),
+                )
+            )
+    for load in loads:
+        load.wait()
+
+    @pl.when(side == 0)
+    def _():
+        picture.start()
+        for copy in late:
+            copy.start()
+
+    @pl.when(side == 1)
+    def _():
+        for which, (table, pack) in enumerate(((near_t, pack_t), (near_c, pack_c))):
+            for o in range(STEPS):
+                for j in range(PACK):
+                    pack[o, j] = table[send_idx[PACK * o + j]]
+                hops[STEPS * which + o][0].start()
+        for copy in own:
+            copy.start()
+        for hop, forward in hops[:STEPS]:
+            hop.wait_recv()
+            forward.start()
+        for copy in late:
+            copy.start()
+        for hop, forward in hops[STEPS:]:
+            hop.wait_recv()
+            forward.start()
+        for hop, forward in hops:
+            hop.wait_send()
+            forward.wait()
+        for copy in own:
+            copy.wait()
+        picture.wait_recv()
+
+    for p in range(half):
+        x[p] = choose(work_idx[p], near_t, far_t)
+        cot[p] = choose(work_idx[p], near_c, far_c)
+
+    @pl.when(side == 0)
+    def _():
+        picture.wait_send()
+
+    for copy in first + late:
+        copy.wait()
+
+
+def route_in(count, send_idx, work_idx, home_t, home_c, qkv, out_w, gen, gen_out, up, down):
+    slots = home_t.shape[0]
+    block = home_t.shape[1:]
+    half = slots // 2
+
+    def like(value):
+        return jax.ShapeDtypeStruct(value.shape, value.dtype)
+
+    weights = (qkv, out_w, gen, gen_out, up, down)
+    rows = jax.ShapeDtypeStruct((half,) + block, BF16)
+    near = pltpu.VMEM((slots,) + block, BF16)
+    far = pltpu.VMEM((2 * STEPS * PACK,) + block, BF16)
+    pack = pltpu.VMEM((STEPS, PACK) + block, BF16)
+    return pl.pallas_call(
+        functools.partial(route_kernel, count),
+        out_shape=[rows, rows, rows] + [like(w) for w in weights],
+        in_specs=[SMEM, SMEM] + [ANY] * 8,
+        out_specs=[VMEM, VMEM] + [ANY] * 7,
+        scratch_shapes=[near, near, far, far, pack, pack]
+        + [pltpu.SemaphoreType.DMA((20,)), pltpu.SemaphoreType.DMA((20,)), pltpu.SemaphoreType.DMA((2,))],
+        compiler_params=pltpu.CompilerParams(vmem_limit_bytes=LIMIT, collective_id=0, has_side_effects=True),
+        name="route_in",
+    )(send_idx, work_idx, home_t, home_c, *weights)
+
+
+class Job:
+    def __init__(self, links, spot, own, other, m, xs, xr, z1s, z1r, z2s, z2r):
+        self.own, self.m, self.xs, self.xr = own, m, xs, xr
+        self.z1s, self.z1r, self.z2s, self.z2r = z1s, z1r, z2s, z2r
+        side, me, c = spot
+        self.rows = own.shape[1] // 8
+        self.bx, self.b1, self.b2 = me % 2, (me // 2) % 2, me // 4
+        flip_x, flip_1, flip_2 = 1 - 2 * self.bx, 2 - 4 * self.b1, 4 - 8 * self.b2
+        self.mp = links.copy(other, m, (side, me, 1 - c))
+        self.hop_x = links.copy(xs, xr, (side, me + flip_x, c))
+        self.hop_1 = links.copy(z1s, z1r, (side, me + flip_1, c))
+        self.hop_2 = links.copy(z2s, z2r, (side, me + flip_2, c))
+
+    def at(self, zz, bx):
+        return pl.ds(pl.multiple_of((2 * zz + bx) * self.rows, self.rows), self.rows)
+
+    def base(self, i, zz, bx):
+        at = self.at(zz, bx)
+        return self.own[i, at, :].astype(F32) + self.m[i, at, :].astype(F32)
+
+    def step_mp(self):
+        self.mp.start()
+
+    def step_x(self):
+        self.mp.wait_recv()
+        for i in range(self.own.shape[0]):
+            for zz in range(4):
+                self.xs[i, zz] = self.base(i, zz, 1 - self.bx).astype(BF16)
+        self.hop_x.start()
+
+    def step_1(self):
+        self.hop_x.wait_recv()
+        for i in range(self.own.shape[0]):
+            for b2 in range(2):
+                zz = 2 * b2 + 1 - self.b1
+                total = self.base(i, zz, self.bx) + self.xr[i, zz].astype(F32)
+                self.z1s[i, b2] = total.astype(BF16)
+        self.hop_1.start()
+
+    def last(self, i, b2):
+        zz = 2 * b2 + self.b1
+        total = self.base(i, zz, self.bx) + self.xr[i, zz].astype(F32)
+        return total + self.z1r[i, b2].astype(F32)
+
+    def step_2(self):
+        self.hop_1.wait_recv()
+        for i in range(self.own.shape[0]):
+            self.z2s[i] = self.last(i, 1 - self.b2).astype(BF16)
+        self.hop_2.start()
+
+    def total(self, i):
+        return self.last(i, self.b2) + self.z2r[i].astype(F32)
+
+    def finish(self):
+        self.hop_2.wait_recv()
+
+    def drain(self):
+        for copy in (self.mp, self.hop_x, self.hop_1, self.hop_2):
+            copy.wait_send()
+
+
+def job_scratch(lead, rows, cols):
+    part = rows // 8
+    return [pltpu.VMEM((lead, rows, cols), BF16)] + [
+        pltpu.VMEM((lead,) + n + (part, cols), BF16) for n in ((4,), (4,), (2,), (2,), (), ())
+    ]
+
+
+def comm_kernel(count, back_idx, home_idx, f_own, f_oth, g_own, g_oth, t_own, t_oth, y_own, r_own, gains, ffn_out, tower_out, cross_out, y_out, r_out, gain_out, *rest):
+    jobs_scratch = [rest[8 * k : 8 * k + 7] + (rest[8 * k + 7],) for k in range(5)]
+    rest = rest[40:]
+    near_y, near_r, far_y, far_r, pack_y, pack_r, cross_low, cross_got, gain_s, gain_r, send_sems, recv_sems, local_sems = rest
+    side, me, c, along = place(count)
+    twin, across = (side, me, 1 - c), (1 - side, me, c)
+    links = Links(send_sems, recv_sems)
+    bx, b1, b2 = me % 2, (me // 2) % 2, me // 4
+    flips = [(side, me + 1 - 2 * bx, c), (side, me + 2 - 4 * b1, c), (side, me + 4 - 8 * b2, c)]
+    chunk = f_own.shape[2] // 3
+    half = y_own.shape[0]
+    slots = 2 * half
+
+    loads, jobs = [], []
+    for k in range(5):
+        own = jobs_scratch[k][7]
+        if k < 3:
+            at = pl.ds(k * chunk, chunk)
+            source, other = f_own.at[:, :, at], f_oth.at[:, :, at]
+        else:
+            source, other = (g_own, g_oth) if k == 3 else (t_own, t_oth)
+        loads.append(pltpu.make_async_copy(source, own, local_sems.at[k]))
+        jobs.append(Job(links, (side, me, c), own, other, *jobs_scratch[k][:7]))
+    loads.append(pltpu.make_async_copy(y_own, near_y.at[pl.ds(0, half)], local_sems.at[5]))
+    loads.append(pltpu.make_async_copy(r_own, near_r.at[pl.ds(0, half)], local_sems.at[6]))
+    for load in loads:
+        load.start()
+    swaps = [
+        links.copy(own, table.at[pl.ds(half, half)], twin) for own, table in ((y_own, near_y), (r_own, near_r))
+    ]
+    hops = []
+    for far, pack in ((far_y, pack_y), (far_r, pack_r)):
+        for o in range(STEPS):
+            there = far.at[pl.ds(PACK * o, PACK)]
+            hops.append(
+                (
+                    links.copy(pack.at[o], there, along(o + 1)),
+                    links.copy(there, far.at[pl.ds(PACK * (STEPS + o), PACK)], twin),
+                )
+            )
+    gain_copies = [links.copy(gain_s.at[k], gain_r.at[k], device) for k, device in enumerate([twin] + flips + [across])]
+    cross_copy = links.copy(cross_low, cross_got, across)
+    greet([twin, across] + flips, [along(k) for k in (-3, -2, -1, 1, 2, 3)], side)
+
+    for swap in swaps:
+        swap.start()
+    for job in jobs[:4]:
+        job.step_mp()
+
+    @pl.when(side == 1)
+    def _():
+        jobs[4].step_mp()
+
+    gain_s[0] = gains[...]
+    gain_copies[0].start()
+    for load in loads:
+        load.wait()
+    for job in jobs[:3]:
+        job.step_x()
+
+    def gain_step(k):
+        gain_copies[k].wait_recv()
+        gain_s[k + 1] = gain_s[k] + gain_r[k]
+        if k < 3:
+            gain_copies[k + 1].start()
+
+    gain_step(0)
+    for swap in swaps:
+        swap.wait_recv()
+
+    @pl.when(side == 1)
+    def _():
+        for which, (table, pack) in enumerate(((near_y, pack_y), (near_r, pack_r))):
+            for o in range(STEPS):
+                for j in range(PACK):
+                    pack[o, j] = table[back_idx[PACK * o + j]]
+                hops[STEPS * which + o][0].start()
+
+    jobs[3].step_x()
+    gain_step(1)
+
+    @pl.when(side == 1)
+    def _():
+        jobs[4].step_x()
+        for hop, forward in hops:
+            hop.wait_recv()
+            forward.start()
+
+    gain_step(2)
+    jobs[0].step_1()
+    jobs[1].step_1()
+    jobs[2].step_1()
+    jobs[0].step_2()
+    jobs[3].step_1()
+    jobs[1].step_2()
+    jobs[2].step_2()
+
+    @pl.when(side == 1)
+    def _():
+        jobs[4].step_1()
+
+    jobs[3].step_2()
+
+    @pl.when(side == 1)
+    def _():
+        jobs[4].step_2()
+
+    gain_step(3)
+
+    @pl.when(side == 1)
+    def _():
+        gain_copies[4].start()
+
+    for k in range(3):
+        jobs[k].finish()
+        for i in range(2):
+            ffn_out[i, :, k * chunk : (k + 1) * chunk] = jobs[k].total(i)
+    jobs[3].finish()
+
+    @pl.when(side == 1)
+    def _():
+        for i in range(4):
+            low = jobs[3].total(i).astype(BF16)
+            cross_low[i] = low
+            cross_out[i] = low.astype(F32)
+        cross_copy.start()
+        jobs[4].finish()
+        for i in range(4):
+            tower_out[i] = jobs[4].total(i)
+        gain_out[...] = gain_s[4]
+        for hop, forward in hops:
+            hop.wait_send()
+            forward.wait()
+
+    @pl.when(side == 0)
+    def _():
+        for i in range(4):
+            tower_out[i] = jobs[3].total(i)
+
+    for s in range(slots):
+        y_out[s] = choose(home_idx[s], near_y, far_y)
+        r_out[s] = choose(home_idx[s], near_r, far_r).astype(F32)
+
+    @pl.when(side == 0)
+    def _():
+        cross_copy.wait_recv()
+        for i in range(4):
+            cross_out[i] = cross_got[i].astype(F32)
+        gain_copies[4].wait_recv()
+        gain_out[...] = gain_s[4]
+        gain_out[2:3, :] = gain_r[4, 2:3, :]
+
+    @pl.when(side == 1)
+    def _():
+        cross_copy.wait_send()
+        gain_copies[4].wait_send()
+        jobs[4].drain()
+
+    for copy in gain_copies[:4] + swaps:
+        copy.wait_send()
+    for job in jobs[:4]:
+        job.drain()
+
+
+def comm(count, back_idx, home_idx, f_own, f_oth, g_own, g_oth, t_own, t_oth, y_own, r_own, gains):
+    lead, width, hidden = f_own.shape
+    part = width // count
+    half, block = y_own.shape[0], y_own.shape[1:]
+    slots = 2 * half
+    scratch = []
+    for k in range(5):
+        shape = (2, width, hidden // 3) if k < 3 else g_own.shape
+        scratch += job_scratch(*shape) + [pltpu.VMEM(shape, BF16)]
+    near = pltpu.VMEM((slots,) + block, BF16)
+    far = pltpu.VMEM((2 * STEPS * PACK,) + block, BF16)
+    pack = pltpu.VMEM((STEPS, PACK) + block, BF16)
+    small = (4, part, g_own.shape[2])
+    scratch += [near, near, far, far, pack, pack, pltpu.VMEM(small, BF16), pltpu.VMEM(small, BF16)]
+    scratch += [pltpu.VMEM((5,) + gains.shape, F32), pltpu.VMEM((5,) + gains.shape, F32)]
+    scratch += [pltpu.SemaphoreType.DMA((40,)), pltpu.SemaphoreType.DMA((40,)), pltpu.SemaphoreType.DMA((7,))]
+    shapes = [
+        ((lead, part, hidden), F32),
+        (small, F32),
+        (small, F32),
+        ((slots,) + block, BF16),
+        ((slots,) + block, F32),
+        (gains.shape, F32),
+    ]
+    return pl.pallas_call(
+        functools.partial(comm_kernel, count),
+        out_shape=[jax.ShapeDtypeStruct(*shape) for shape in shapes],
+        in_specs=[SMEM, SMEM] + [ANY] * 8 + [VMEM],
+        out_specs=[VMEM] * 6,
+        scratch_shapes=scratch,
+        compiler_params=pltpu.CompilerParams(vmem_limit_bytes=60 * 1024 * 1024, collective_id=1, has_side_effects=True),
+        name="comm",
+    )(back_idx, home_idx, f_own, f_oth, g_own, g_oth, t_own, t_oth, y_own, r_own, gains)
+
+
 def swap_mp(value, captions_only=False):
     if not captions_only:
         return lax.ppermute(value, "mp", [(0, 1), (1, 0)])
@@ -530,25 +948,31 @@
         other = [swap_mp(g, True) for g in got]
         return gather_slots(work_idx, [table] + got + other, [per_core])[0].reshape(rows, width)
 
-    got_tokens = travel(home_tokens)
-    image_rows = lax.dynamic_slice_in_dim(tokens[0], c * rows, rows)
+    fused = count == 8 and width % (count * 32) == 0
     pairs = [(2 * d + k, 2 * (count + d) + k) for d in range(count) for k in range(2)]
-    image_here = lax.ppermute(image_rows, ("half", "dp", "mp"), pairs)
-    got_cot = travel(home_cot)
 
     qkv = jnp.transpose(qkv_weight[0], (1, 0, 2))
     cross = jnp.stack([cross_query_matrix, cross_keyval[:, 0], cross_keyval[:, 1]])
     gen_own = jnp.where(is_image, qkv, cross)
     gen_out_own = jnp.where(is_image, out_weight[0], cross_out)
-    gen_oth = swap_mp(gen_own)
-    gen_out_oth = swap_mp(gen_out_own)
-    qkv_oth = swap_mp(qkv, True)
-    out_oth = swap_mp(out_weight[0], True)
-    up_oth = swap_mp(up_weight[0])
-    down_oth = swap_mp(down_weight[0])
-
-    x = settle(home_tokens, got_tokens)
-    cot = settle(home_cot, got_cot)
+    if fused:
+        x, cot, image_here, qkv_oth, out_oth, gen_oth, gen_out_oth, up_oth, down_oth = route_in(
+            count, send_idx, work_idx, home_tokens, home_cot, qkv, out_weight[0], gen_own, gen_out_own, up_weight[0], down_weight[0]
+        )
+        x, cot, image_here = (value.reshape(rows, width) for value in (x, cot, image_here))
+    else:
+        got_tokens = travel(home_tokens)
+        image_rows = lax.dynamic_slice_in_dim(tokens[0], c * rows, rows)
+        image_here = lax.ppermute(image_rows, ("half", "dp", "mp"), pairs)
+        got_cot = travel(home_cot)
+        gen_oth = swap_mp(gen_own)
+        gen_out_oth = swap_mp(gen_out_own)
+        qkv_oth = swap_mp(qkv, True)
+        out_oth = swap_mp(out_weight[0], True)
+        up_oth = swap_mp(up_weight[0])
+        down_oth = swap_mp(down_weight[0])
+        x = settle(home_tokens, got_tokens)
+        cot = settle(home_cot, got_cot)
     gains = norm_gains[0]
     gain_cross = cross_gain[None]
     heads_shape = ((6, rows, 128), BF16)
@@ -573,9 +997,7 @@
         meta, a, b, r, gains, gen_own, gen_oth, gen_out_own, gen_out_oth,
     )
     ffn_g_oth, acc_out, acc_grad = ffn_call(False, ffn_in, cot, up_oth, down_oth)
-    ffn_arrived = swap_mp(ffn_g_oth)
     ffn_g_own, y, gm, gain_ffn = ffn_call(True, ffn_in, cot, up_weight[0], down_weight[0], acc_out, acc_grad, mixed, gains)
-    ffn_sum = reduce_dp(ffn_g_own, ffn_arrived)
 
     g_own, g_oth, da, db = call(
         back_kernel,
@@ -585,7 +1007,6 @@
         True,
         meta, gm, ctx, sums, q, k, v, a, b, gen_own, gen_oth, gen_out_own, gen_out_oth,
     )
-    gen_sum = reduce_dp(g_own, swap_mp(g_oth))
     image_part = lax.ppermute(db.astype(BF16), ("half", "dp", "mp"), [(d, s) for s, d in pairs])
 
     gt, g3_own, g3_oth, gain_two = call(
@@ -596,36 +1017,49 @@
         True,
         meta, x, gains, gain_cross, gm, da, db, r, normed, sq, sk, sv, st, qkv, qkv_oth, out_weight[0], out_oth,
     )
-    cap_sum = reduce_dp(g3_own, swap_mp(g3_oth))
     grad_rows = jnp.where(is_image, gt + image_part.astype(F32), gt).astype(BF16)
 
-    def go_home(values):
-        own = values.reshape(per_core, SLOT, width)
-        other = swap_mp(own)
-        packs = gather_slots(back_idx, [own, other], [QCAP // 2] * (SPREAD - 1))
-        got = [caption_shift(pack, o + 1) for o, pack in enumerate(packs)]
-        more = [swap_mp(g, True) for g in got]
-        return gather_slots(home_idx, [own, other] + got + more, [cap_dev])[0].reshape(row_count, width)
-
-    layer_out = go_home(y)
-    grad_tokens = go_home(grad_rows).astype(F32)
-
-    zero = jnp.zeros_like(gain_ffn)
-    mine = jnp.concatenate([gain_two[0:1], gain_ffn])
-    none = jnp.zeros_like(mine)
-    gain_rows = jnp.concatenate(
-        [jnp.where(is_image, mine, none), jnp.where(is_image, none, mine), gain_two[1:2]]
-    )
-    gain_rows = lax.psum(gain_rows, ("half", "dp", "mp"))
-    part = width // count
-    gain_rows = lax.dynamic_slice_in_dim(gain_rows, me * part, part, axis=1)
-    sum_gains = jnp.where(is_image, gain_rows[0:2], gain_rows[2:4])
-    sum_cross_gain = gain_rows[4]
-
-    cross_low = gen_sum.astype(BF16)
-    cross_arrived = lax.ppermute(cross_low, ("half", "dp", "mp"), [(d, s) for s, d in pairs])
-    cross_sum = jnp.where(is_image, cross_arrived, cross_low).astype(F32)
-    tower_sum = jnp.where(is_image, gen_sum, cap_sum)
+    if fused:
+        gain_mine = jnp.concatenate([gain_two[0:1], gain_ffn, gain_two[1:2], jnp.zeros((5, width), F32)])
+        ffn_sum, tower_sum, cross_sum, layer_out, grad_tokens, gain_rows = comm(
+            count, back_idx, home_idx, ffn_g_own, ffn_g_oth, g_own, g_oth, g3_own, g3_oth,
+            y.reshape(per_core, SLOT, width), grad_rows.reshape(per_core, SLOT, width), gain_mine,
+        )
+        layer_out, grad_tokens = layer_out.reshape(row_count, width), grad_tokens.reshape(row_count, width)
+        gain_rows = lax.dynamic_slice_in_dim(gain_rows, me * (width // count), width // count, axis=1)
+        sum_gains, sum_cross_gain = gain_rows[0:2], gain_rows[2]
+    else:
+        ffn_sum = reduce_dp(ffn_g_own, swap_mp(ffn_g_oth))
+        gen_sum = reduce_dp(g_own, swap_mp(g_oth))
+        cap_sum = reduce_dp(g3_own, swap_mp(g3_oth))
+
+        def go_home(values):
+            own = values.reshape(per_core, SLOT, width)
+            other = swap_mp(own)
+            packs = gather_slots(back_idx, [own, other], [QCAP // 2] * (SPREAD - 1))
+            got = [caption_shift(pack, o + 1) for o, pack in enumerate(packs)]
+            more = [swap_mp(g, True) for g in got]
+            return gather_slots(home_idx, [own, other] + got + more, [cap_dev])[0].reshape(row_count, width)
+
+        layer_out = go_home(y)
+        grad_tokens = go_home(grad_rows).astype(F32)
+
+        zero = jnp.zeros_like(gain_ffn)
+        mine = jnp.concatenate([gain_two[0:1], gain_ffn])
+        none = jnp.zeros_like(mine)
+        gain_rows = jnp.concatenate(
+            [jnp.where(is_image, mine, none), jnp.where(is_image, none, mine), gain_two[1:2]]
+        )
+        gain_rows = lax.psum(gain_rows, ("half", "dp", "mp"))
+        part = width // count
+        gain_rows = lax.dynamic_slice_in_dim(gain_rows, me * part, part, axis=1)
+        sum_gains = jnp.where(is_image, gain_rows[0:2], gain_rows[2:4])
+        sum_cross_gain = gain_rows[4]
+
+        cross_low = gen_sum.astype(BF16)
+        cross_arrived = lax.ppermute(cross_low, ("half", "dp", "mp"), [(d, s) for s, d in pairs])
+        cross_sum = jnp.where(is_image, cross_arrived, cross_low).astype(F32)
+        tower_sum = jnp.where(is_image, gen_sum, cap_sum)
     return (
         layer_out[None],
         grad_tokens[None],

time: 786 us -> 417 us (0.53)
  waiting for transfers between devices: 146 us -> 0.01 us
  starting transfers between devices: 96.5 us -> 1.35 us
  blocking collectives: 62.5 us -> 0 us
  Pallas kernels: 415 us -> 373 us
  other arithmetic: 38.1 us -> 15.3 us
    ppermute x46 -> x0, waiting for transfers between devices: 127 us -> none  [the longest x12 61.8 us: caption_shift(): return lax.ppermute(value, ('half', 'dp', 'mp'), pairs)]
    ppermute x46 -> x0, starting transfers between devices: 94.7 us -> none  [the longest x12 41.5 us: caption_shift(): return lax.ppermute(value, ('half', 'dp', 'mp'), pairs)]
    psum x1 -> x0, blocking collectives: 62.5 us -> none  [shards(): gain_rows = lax.psum(gain_rows, ('half', 'dp', 'mp'))]
    pallas_call x8 -> x2, Pallas kernels: 283 us -> 241 us  [the longest x1 196 us: comm(): pl.pallas_call(functools.partial(comm_kernel, count), out_shape=[jax.Shap...]
    ppermute x1, waiting for transfers between devices: 18.9 us -> 0.01 us  [shards(): lax.ppermute(db.astype(BF16), ('half', 'dp', 'mp'), [(d, s) for s, d in p...]
    convert_element_type x12 -> x0, other arithmetic: 17.5 us -> none  [the longest x9 15.1 us: reduce_dp(): send = (part(kept, 1 - mine) + part(got, 1 - mine)).astype(BF16)]
  transfers between devices with their start and end apart: 47 -> 1, of which waited for: 11 -> 0; matrix products, arithmetic and copies ran while one was open for 6% -> 1% of each run, Pallas kernels for 48% -> 8%
where the time goes in v2:
time: 417 us; the launch traced here: 410 us
  Pallas kernels  373 us (89%)
  local copies, waits for them, and re-layouts  19.3 us (5%)
  other arithmetic  15.3 us (4%)
    pallas_call x1, Pallas kernels, comm(): pl.pallas_call(functools.partial(comm_kernel, count), out_shape=[jax.Shap...  196 us
    pallas_call x4, Pallas kernels, call(): pl.pallas_call(kernel, out_shape=[jax.ShapeDtypeStruct(shape, dtype) for...  101 us
    pallas_call x1, Pallas kernels, route_in(): pl.pallas_call(functools.partial(route_kernel, count), out_shape=[rows, r...  45 us
    pallas_call x2, Pallas kernels, ffn_call(): pl.pallas_call(functools.partial(ffn_kernel, last), grid=(3,), out_shape=...  30.7 us
  transfers between devices with their start and end apart: 1, of which 0 were waited for; matrix products, arithmetic and copies ran while one was open for 1% of the time, Pallas kernels for 8%

profile of v2, /device:TPU:4, one launch (start us, length us, event | category | flops | bytes accessed | tf_op | source)
XLA Modules:
  0.0 410.2 jit_solution(13440199314451581732)
XLA Ops:
  0.7 0.7 compare_and_fusion.1
  1.4 0.7 fusion.9
  2.1 0.9 convert_reduce_fusion
  3.8 0.6 eq.181
  5.1 3.8 fusion.20
  10.3 0.7 pad_add_fusion.meta
  12.2 0.9 broadcast_select_fusion.gen_out.o_own
  13.1 1.6 maximum_select_fusion.gen.w_own
  14.8 0.7 select_reduce_fusion.1
  15.5 45.0 %route_in.1 = (bf16[9,64,768]{2,1,0:T(8,128)(2,1)}, bf16[9,64,768]{2,1,0:T(8,128)(2,1)}, bf16[9,64,768]{2,1,0:T(8,128)(2,1)}, bf16[3,768,384]{2,1,0:T(8,128)(2,1...) custom-call(s32[9]{0:T(128)} %get-tuple-element.121.send_idx, ...), custom_call_target="tpu_custom_call" | custom-call | tf_op jit(solution)/shard_map/route_in/pallas_call | solution.py:536
  60.5 20.4 %pre.1 = (bf16[576,768]{1,0:T(8,128)(2,1)}, f32[576,768]{1,0:T(8,128)}, bf16[576,768]{1,0:T(8,128)(2,1)}, bf16[6,576,128]{2,1,0:T(8,128)(2,1)}, bf16[6,576,128]{...) custom-call(s32[10]{0:T(128)} %pad_add_fusion.meta, bf16[576,768]{1,0:T(8,128)(2,1)} %bitcast.68, ...), custom_call_target="tpu_custom_call" | custom-call | tf_op jit(solution)/shard_map/pre/pallas_call | solution.py:351
  80.9 1.1 bitcast_select_fusion.b_ref
  82.0 18.9 %mid.1 = (bf16[6,576,128]{2,1,0:T(8,128)(2,1)}, bf16[6,576,128]{2,1,0:T(8,128)(2,1)}, bf16[6,576,128]{2,1,0:T(8,128)(2,1)}, bf16[6,576,128]{2,1,0:T(8,128)(2,1)}...) custom-call(s32[10]{0:T(128)} %pad_add_fusion.meta, ...), custom_call_target="tpu_custom_call" | custom-call | tf_op jit(solution)/shard_map/mid/pallas_call | solution.py:351
  100.9 13.5 %ffn_other.1 = (bf16[2,768,1536]{2,1,0:T(8,128)(2,1)}, f32[576,768]{1,0:T(8,128)}, f32[576,768]{1,0:T(8,128)}) custom-call(bf16[576,768]{1,0:T(8,128)(2,1)} %get-tuple-element.63.f_ref, bf16[576,768]{1,0:T(8,128)(2,1)} %bitcast.65, bf16[768,1536]{1,0:T(8,128)(2,1)} %get-tuple-element.65.up, bf16[1536,768]{1,0:T(8,128)(2,1)} %get-tuple-element.66.down), custom_call_target="tpu_custom_call" | custom-call | tf_op jit(solution)/shard_map/ffn_other/pallas_call | solution.py:385
  114.4 17.2 %ffn_own.1 = (bf16[2,768,1536]{2,1,0:T(8,128)(2,1)}, bf16[576,768]{1,0:T(8,128)(2,1)}, f32[576,768]{1,0:T(8,128)}, f32[1,768]{1,0:T(1,128)}) custom-call(bf16[576,768]{1,0:T(8,128)(2,1)} %get-tuple-element.63.f_ref, bf16[576,768]{1,0:T(8,128)(2,1)} %bitcast.66, bf16[768,1536]{1,0:T(8,128)(2,1)} %bitcast.62, bf16[1536,768]{1,0:T(8,128)(2,1)} %bitcast.64, ...), custom_call_target="tpu_custom_call" | custom-call | tf_op jit(solution)/shard_map/ffn_own/pallas_call | solution.py:385
  131.6 28.5 %back.1 = (bf16[4,768,384]{2,1,0:T(8,128)(2,1)}, bf16[4,768,384]{2,1,0:T(8,128)(2,1)}, f32[576,768]{1,0:T(8,128)}, f32[576,768]{1,0:T(8,128)}) custom-call(s32[10]{0:T(128)} %pad_add_fusion.meta, f32[576,768]{1,0:T(8,128)} %get-tuple-element.72.gm_ref, bf16[6,576,128]{2,1,0:T(8,128)(2,1)} %get-tuple-element.73.c_ref, f32[12,1,576]{2,1,0:T(1,128)} %get-tuple-element.74.s_ref, ...), custom_call_target="tpu_custom_call" | custom-call | tf_op jit(solution)/shard_map/back/pallas_call | solution.py:351
  160.1 1.6 convert_element_type.17
  161.7 1.3 collective-permute-start
  163.1 33.1 %post.1 = (f32[576,768]{1,0:T(8,128)}, bf16[4,768,384]{2,1,0:T(8,128)(2,1)}, bf16[4,768,384]{2,1,0:T(8,128)(2,1)}, f32[2,768]{1,0:T(2,128)}) custom-call(s32[10]{0:T(128)} %pad_add_fusion.meta, bf16[576,768]{1,0:T(8,128)(2,1)} %bitcast.69, f32[2,768]{1,0:T(2,128)} %bitcast.79, f32[1,768]{1,0:T(1,128)} %broadcast_in_dim.126.gain_cross, ...), custom_call_target="tpu_custom_call" | custom-call | tf_op jit(solution)/shard_map/post/pallas_call | solution.py:351
  196.8 0.8 fusion.21
  197.6 0.7 maximum_maximum_fusion.gains
  198.3 2.6 fusion
  200.9 196.4 %comm.1 = (f32[2,96,1536]{2,1,0:T(8,128)}, f32[4,96,384]{2,1,0:T(8,128)}, f32[4,96,384]{2,1,0:T(8,128)}, bf16[18,64,768]{2,1,0:T(8,128)(2,1)}, f32[18,64,768]{2,1,0:T(8,128)}, /*index=5*/f32[8,768]{1,0:T(8,128)}) custom-call(s32[9]{0:T(128)} %get-tuple-element.122.back_idx, s32[18]{0:T(128)} %broadcast_select_fusion.2.home_idx, ...), custom_call_target="tpu_custom_call" | custom-call | tf_op jit(solution)/shard_map/comm/pallas_call | solution.py:804
  397.4 1.9 slice_bitcast_fusion.1
  399.3 1.6 slice_bitcast_fusion.6
  400.9 0.8 constant_dynamic-slice_fusion
  402.7 1.1 slice_bitcast_fusion
  403.8 0.7 slice_bitcast_fusion.2
  404.6 0.9 copy.29
  405.5 1.2 copy.36
  406.7 1.4 copy-done.2
  408.2 1.8 copy.37
  (63 shorter events, 5.9 us)
Async XLA Ops:
  4.6 0.5 copy-start.18
  5.1 3.8 copy-start.12
  5.1 4.4 %copy-start.9 = (s32[144]{0:T(256)S(1)}, s32[144]{0:T(256)}, u32[]{:S(2)}) copy-start(s32[144]{0:T(256)} %param.23) | copy-start | bytes 1732
  5.1 5.0 %copy-start.13 = (s32[144]{0:T(256)S(1)}, s32[144]{0:T(256)}, u32[]{:S(2)}) copy-start(s32[144]{0:T(256)} %param.24) | copy-start | bytes 1732
  10.9 1.1 copy-start.1
  10.9 1.2 copy-start.7
  10.9 2.1 copy-start.8
  11.1 1.9 copy-start
  13.0 1.7 copy-start.10
  13.0 1.7 copy-start.11
  13.1 1.7 copy-start.16
  13.1 1.7 copy-start.17
  13.1 1.7 copy-start.19
  13.1 1.7 copy-start.20
  60.5 20.4 %copy-start.5 = (bf16[9,64,768]{2,1,0:T(8,128)(2,1)S(1)}, bf16[9,64,768]{2,1,0:T(8,128)(2,1)}, u32[]{:S(2)}) copy-start(bf16[9,64,768]{2,1,0:T(8,128)(2,1)} %get-tuple-element.59) | copy-start | bytes 2654212
  161.7 36.6 %collective-permute-start = (bf16[576,768]{1,0:T(8,128)(2,1)S(1)}, bf16[576,768]{1,0:T(8,128)(2,1)S(1)}, u32[]{:S(2)}, u32[]{:S(2)}) collective-permute-start(bf16[576,768]{1,0:T(8,128)(2,1)S(1)} %convert_element_type.17), channel_id=1, source_target_pairs={{16,0},{17,1},{18,2},{19,3},{20,4},{21,5},{22,6},{23,7},{24,8},{25... | collective-permute-start | bytes 2654216 | tf_op jit(solution)/shard_map/ppermute | solution.py:1010
  163.1 33.1 %copy-start.15 = (s32[144]{0:T(256)S(1)}, s32[144]{0:T(256)}, u32[]{:S(2)}) copy-start(s32[144]{0:T(256)} %get-tuple-element.129) | copy-start | bytes 1732
  163.1 34.5 %copy-start.14 = (f32[1,768]{1,0:T(1,128)S(1)}, f32[1,768]{1,0:T(1,128)}, u32[]{:S(2)}) copy-start(f32[1,768]{1,0:T(1,128)} %get-tuple-element.92) | copy-start | bytes 9220
  397.3 5.4 %copy-start.4 = (f32[2,96,1536]{2,1,0:T(8,128)S(1)}, f32[2,96,1536]{2,1,0:T(8,128)}, u32[]{:S(2)}) copy-start(f32[2,96,1536]{2,1,0:T(8,128)} %get-tuple-element.96) | copy-start | bytes 3538948
  397.4 6.5 %copy-start.6 = (f32[4,96,384]{2,1,0:T(8,128)S(1)}, f32[4,96,384]{2,1,0:T(8,128)}, u32[]{:S(2)}) copy-start(f32[4,96,384]{2,1,0:T(8,128)} %get-tuple-element.98) | copy-start | bytes 1769476
  403.8 1.7 copy-start.3
  405.5 2.6 copy-start.2
